TPU v7x, 512 devices: a whole 4x8x8 slice. The times are simulated.
512 devices in a mesh: seq: 128 (over z_lo, y, x), ch: 4 (over z_hi, core).
Axes of the slice: x: 4, y: 8, z: 8 (z_hi: 2, z_lo: 4; z = z_hi * 4 + z_lo), core: 2. Of those that a mesh axis runs over, the one named last changes fastest.
Arguments:
- tokens: bfloat16 [16384, 512], P('seq', 'ch'), may hold values from -36 to 36
- gain_mix: float32 [512], replicated, may hold values from 0.1 to 1.9
- w_in: bfloat16 [3, 512, 512], P(None, None, 'ch'), may hold values from -0.25 to 0.25
- short_w: float32 [3, 3, 512], P(None, None, 'ch'), may hold values from -3.5 to 3.5
- filters: bfloat16 [2, 512, 16384], P(None, 'ch', 'seq'), may hold values from -0.046875 to 0.046875
- conv_bias: float32 [2, 512], P(None, 'ch'), may hold values from 0.5 to 1.5
- w_out: bfloat16 [512, 512], P('ch'), may hold values from -0.25 to 0.25
- gain_mlp: float32 [512], replicated, may hold values from 0.1 to 1.9
- w_up: bfloat16 [512, 2048], P(None, 'ch'), may hold values from -0.25 to 0.25
- w_down: bfloat16 [2048, 512], P('ch'), may hold values from -0.125 to 0.125
Outputs:
- result: bfloat16 [16384, 512], P('seq', 'ch')
All inputs are finite; a program needn't handle non-finite values.
Results may differ from a plain program's by a relative error of at most 0.018.
Values may be sent and summed in bfloat16 or wider, within the bound.
No kernel may reach another device: no remote copies, remote signals or barrier semaphores. Data moves between devices by JAX's collectives and lax.ppermute only.
A program may use at most 64 MiB of HBM per device.

v0:
```python
import jax
import jax.numpy as jnp
import ml_dtypes
import numpy as np
from jax import lax
from jax.experimental import pallas as pl
from jax.experimental.pallas import tpu as pltpu
from jax.sharding import Mesh, PartitionSpec as P

epsilon = 1e-06

SEQ = ("z", "y", "x")
CH = ("h", "c")


def rms_norm(values, gain):
    wide = values.astype(jnp.float32)
    scale = lax.rsqrt(jnp.mean(wide * wide, axis=-1, keepdims=True) + epsilon)
    return (wide * scale * gain).astype(jnp.bfloat16)


def halves_of(table):
    high = table.astype(ml_dtypes.bfloat16)
    low = (table - high.astype(np.float64)).astype(ml_dtypes.bfloat16)
    return high, low


def transform_tables(rows, cols):
    size = rows * cols
    row = np.arange(rows, dtype=np.float64)
    col = np.arange(cols, dtype=np.float64)
    outer_angle = 2.0 * np.pi * (((row[:, None] + 0.25) * row[None, :]) % rows) / rows
    inner_angle = 2.0 * np.pi * ((col[:, None] * col[None, :]) % cols) / cols
    turn_angle = 2.0 * np.pi * (row[:, None] + 0.25) * col[None, :] / size
    outer = np.concatenate([np.cos(outer_angle), -np.sin(outer_angle)], axis=0)
    cos, sin = np.cos(inner_angle), np.sin(inner_angle)
    inner = np.block([[cos, -sin], [sin, cos]])
    outer_high, outer_low = halves_of(outer)
    inner_high, inner_low = halves_of(inner)
    back_high, back_low = halves_of(outer.T / size)
    return (
        np.concatenate([outer_high, outer_low], axis=1),
        inner_high,
        inner_low,
        back_high,
        back_low,
        np.cos(turn_angle).astype(np.float32),
        -np.sin(turn_angle).astype(np.float32),
    )


def dot(left, right):
    return jnp.dot(left, right, preferred_element_type=jnp.float32)


def split(values):
    high = values.astype(jnp.bfloat16)
    return high, (values - high.astype(jnp.float32)).astype(jnp.bfloat16)


def dot_split(values, high_table, low_table):
    high, low = split(values)
    rows = values.shape[0]
    both = dot(jnp.concatenate([high, low], axis=0), high_table)
    return both[:rows] + both[rows:] + dot(high, low_table)


def delayed(values, by):
    rows, cols = values.shape
    turned = pltpu.roll(values, by, 1)
    above = pltpu.roll(turned, 1, 0)
    row = lax.broadcasted_iota(jnp.int32, (rows, cols), 0)
    col = lax.broadcasted_iota(jnp.int32, (rows, cols), 1)
    return jnp.where(col >= by, turned, jnp.where(row >= 1, above, 0.0))


def round_bf16(values):
    return values.astype(jnp.bfloat16).astype(jnp.float32)


def channel_kernel(
    scalars, u, outer, inner_high, inner_low, back_high, back_low, turn_real, turn_imag, mixed
):
    rows, cols = u.shape[1], u.shape[2]

    def short(k):
        values = u[k].astype(jnp.float32)
        total = scalars[3 * k] * values
        total = total + scalars[3 * k + 1] * delayed(values, 1)
        total = total + scalars[3 * k + 2] * delayed(values, 2)
        return total.astype(jnp.bfloat16)

    def forward(signals):
        count = len(signals)
        side = jnp.concatenate(signals, axis=1) if count > 1 else signals[0]
        first = dot(outer[...], jnp.concatenate([side, side], axis=0))
        turned = []
        for k in range(count):
            real = first[:rows, k * cols : (k + 1) * cols]
            imag = first[rows:, k * cols : (k + 1) * cols]
            turned.append(
                jnp.concatenate(
                    [
                        real * turn_real[...] - imag * turn_imag[...],
                        real * turn_imag[...] + imag * turn_real[...],
                    ],
                    axis=1,
                )
            )
        stacked = jnp.concatenate(turned, axis=0) if count > 1 else turned[0]
        spectra = dot_split(stacked, inner_high[...], inner_low[...])
        return [
            (spectra[k * rows : (k + 1) * rows, :cols], spectra[k * rows : (k + 1) * rows, cols:])
            for k in range(count)
        ]

    def inverse(one, two):
        real = one[0] * two[0] - one[1] * two[1]
        negated = -one[0] * two[1] - one[1] * two[0]
        inner = dot_split(
            jnp.concatenate([real, negated], axis=1), inner_high[...], inner_low[...]
        )
        real, negated = inner[:, :cols], inner[:, cols:]
        turned = jnp.concatenate(
            [
                real * turn_real[...] - negated * turn_imag[...],
                -negated * turn_real[...] - real * turn_imag[...],
            ],
            axis=0,
        )
        high, low = split(turned)
        side = dot(back_high[...], jnp.concatenate([high, low], axis=1))
        return side[:, :cols] + side[:, cols:] + dot(back_low[...], high)

    v = short(0)
    signal, response_one, response_two = forward([v, u[3], u[4]])
    first = inverse(signal, response_one) + scalars[9] * v.astype(jnp.float32)
    gated = (short(1).astype(jnp.float32) * round_bf16(first)).astype(jnp.bfloat16)
    (signal,) = forward([gated])
    second = inverse(signal, response_two) + scalars[10] * gated.astype(jnp.float32)
    mixed[...] = (short(2).astype(jnp.float32) * round_bf16(second)).astype(jnp.bfloat16)


def channel_work(u, scalars):
    _, rows, cols = u.shape
    tables = [jnp.asarray(table) for table in transform_tables(rows, cols)]
    vmem = pl.BlockSpec(memory_space=pltpu.VMEM)
    return pl.pallas_call(
        channel_kernel,
        out_shape=jax.ShapeDtypeStruct((rows, cols), jnp.bfloat16),
        in_specs=[pl.BlockSpec(memory_space=pltpu.SMEM)] + [vmem] * (1 + len(tables)),
        out_specs=vmem,
        compiler_params=pltpu.CompilerParams(vmem_limit_bytes=16 * 2**20),
        cost_estimate=pl.CostEstimate(flops=2**29, bytes_accessed=2**20, transcendentals=0),
    )(scalars, u, *tables)


def other_half_pairs():
    pairs = []
    for z in range(8):
        there = (z + 2) % 8
        if there // 4 == z // 4:
            there = (z - 2) % 8
        pairs.append((z % 4 * 2 + z // 4, there % 4 * 2 + there // 4))
    return pairs


def whole_w_out(w_out):
    other = lax.ppermute(w_out, ("z", "h"), other_half_pairs())
    low = lax.axis_index("h") == 0
    halves = jnp.stack([jnp.where(low, w_out, other), jnp.where(low, other, w_out)], axis=1)
    return lax.all_gather(halves, "c", axis=0).reshape(-1, w_out.shape[1])


def local(tokens, gain_mix, w_in, short_w, filters, conv_bias, w_out, gain_mlp, w_up, w_down):
    samples, width = tokens.shape
    shards = lax.axis_size(SEQ)
    whole = lax.all_gather(tokens, CH, axis=1, tiled=True)
    normed = rms_norm(whole, gain_mix)
    projected = jnp.einsum("td,kde->ekt", normed, w_in, preferred_element_type=jnp.float32).astype(
        jnp.bfloat16
    )
    outgoing = jnp.concatenate([projected, filters.transpose(1, 0, 2)], axis=1)
    arrived = lax.all_to_all(outgoing, SEQ, split_axis=0, concat_axis=0, tiled=True)
    w_out_whole = whole_w_out(w_out)
    mine = lax.axis_index(SEQ)
    scalars = lax.dynamic_index_in_dim(
        jnp.concatenate([short_w.reshape(-1, width), conv_bias], axis=0), mine, 1, keepdims=False
    )
    mixed = channel_work(arrived.transpose(1, 0, 2), scalars)
    doubled = jnp.repeat(mixed.reshape(shards, samples), 2, axis=0)
    returned = lax.all_to_all(doubled, SEQ + ("h",), split_axis=0, concat_axis=0, tiled=True)
    both = lax.all_gather(returned, "c", axis=0, tiled=True)
    share = lax.dot_general(
        both, w_out_whole, (((0,), (0,)), ((), ())), preferred_element_type=jnp.float32
    )
    middle = (whole.astype(jnp.float32) + share).astype(jnp.bfloat16)
    normed_mlp = rms_norm(middle, gain_mlp)
    hidden = jax.nn.gelu(jnp.dot(normed_mlp, w_up, preferred_element_type=jnp.float32)).astype(
        jnp.bfloat16
    )
    partial = jnp.dot(hidden, w_down, preferred_element_type=jnp.float32).astype(jnp.bfloat16)
    pieces = partial.reshape(samples, -1, width).transpose(1, 0, 2)
    pieces = lax.all_to_all(pieces, CH, split_axis=0, concat_axis=0, tiled=True)
    total = jnp.sum(pieces.astype(jnp.float32), axis=0)
    own = lax.dynamic_slice_in_dim(middle, lax.axis_index(CH) * width, width, 1)
    return (own.astype(jnp.float32) + total).astype(jnp.bfloat16)


def solution(mesh):
    fine = Mesh(mesh.devices.reshape(4, 8, 4, 2, 2), SEQ + CH)
    return jax.shard_map(
        local,
        mesh=fine,
        in_specs=(
            P(SEQ, CH),
            P(),
            P(None, None, CH),
            P(None, None, CH),
            P(None, CH, SEQ),
            P(None, CH),
            P(CH, None),
            P(),
            P(None, CH),
            P(CH, None),
        ),
        out_specs=P(SEQ, CH),
        check_vma=False,
    )
```

profile of v0, /device:TPU:1, one launch (start us, length us, event | category | flops | bytes accessed | tf_op | source)
XLA Modules:
  0.0 96.5 jit_solution(8971499720807911985)
XLA Ops:
  0.0 0.0 copy-start
  0.0 11.6 %collective-permute-start = (bf16[128,512]{1,0:T(8,128)(2,1)}, bf16[128,512]{1,0:T(8,128)(2,1)S(1)}, u32[]{:S(2)}, u32[]{:S(2)}) collective-permute-start(bf16[128,512]{1,0:T(8,128)(2,1)} %param.23), channel_id=1, source_target_pairs={{0,258},{128,386},{256,2},{384,130},{2,256},{130,384},{258,0},{386... | collective-permute-start | bytes 393224 | tf_op jit(solution)/shard_map/ppermute | solution.py:169
  11.6 13.2 %all_gather.12 = bf16[128,512]{1,0:T(8,128)(2,1)S(1)} all-gather(bf16[128,128]{1,0:T(8,128)(2,1)} %param.17), channel_id=1, replica_groups=mesh['z'=4,'y'=8,'x'=4,'h'=2,'c'=2] {'h','c'}, dimensions={1}, use_global_device_ids=true | all-gather | bytes 163840 | tf_op jit(solution)/shard_map/all_gather | solution.py:178
  24.8 0.1 fusion.6
  24.9 0.6 copy-done.11
  25.5 1.3 %fusion.2 = bf16[128,3,128]{0,2,1:T(8,128)(2,1)S(1)} fusion(bf16[3,512,128]{2,1,0:T(8,128)(2,1)} %param.19, bf16[128,512]{1,0:T(8,128)(2,1)S(1)} %all_gather.12, f32[512]{0:T(512)S(1)} %copy-done.11, f32[128]{0:T(128)S(1)} %add_rsqrt_fusion.1), kind=kOutput, calls=%fused_computation.5 | convolution fusion | flops 50642944 | bytes 625152 | tf_op jit(solution)/shard_map/td,kde->ekt/dot_general | solution.py:180
  26.8 0.0 copy-done.9
  26.8 0.1 copy.30
  26.9 0.9 copy.31
  27.8 11.6 %all-to-all-start = ((bf16[128,5,128]{2,1,0:T(8,128)(2,1)}), bf16[128,5,128]{2,1,0:T(8,128)(2,1)S(1)}, u32[]{:S(2)}, u32[]{:S(2)}) async-start(bf16[128,5,128]{2,1,0:T(8,128)(2,1)} %copy.31), calls=%async_computation | async-start | bytes 524288 | tf_op jit(solution)/shard_map/all_to_all | solution.py:184
  39.5 0.0 copy-start.10
  39.5 0.7 copy-done.10
  40.2 0.7 copy-done.12
  40.9 0.2 fusion.37.scalars
  41.0 0.0 collective-permute-done
  41.0 0.0 copy-done.8
  41.1 0.0 copy-start.4
  41.1 0.0 copy-start.5
  41.1 0.0 copy-start.6
  41.1 0.0 copy-start.7
  41.2 0.0 copy-start.1
  41.2 0.0 copy-start.2
  41.2 0.0 copy-start.3
  41.2 12.1 %all-to-all-done = bf16[128,5,128]{2,1,0:T(8,128)(2,1)S(1)} async-done(((bf16[128,5,128]{2,1,0:T(8,128)(2,1)}), bf16[128,5,128]{2,1,0:T(8,128)(2,1)S(1)}, u32[]{:S(2)}, u32[]{:S(2)}) %all-to-all-start) | async-done | bytes 163872 | tf_op jit(solution)/shard_map/all_to_all | solution.py:184
  53.3 0.0 copy-done.4
  53.3 0.0 copy-done.5
  53.3 0.0 copy-done.6
  53.3 0.0 copy-done.7
  53.4 0.0 copy-done.1
  53.4 0.0 copy-done.2
  53.4 0.0 copy-done.3
  53.4 2.4 %shard_map.163 = bf16[128,128]{1,0:T(8,128)(2,1)S(1)} custom-call(f32[11]{0:T(128)S(1)} %fusion.37.scalars, bf16[5,128,128]{2,1,0:T(8,128)(2,1)S(1)} %bitcast.31, bf16[256,256]{1,0:T(8,128)(2,1)S(1)} %copy-done.1, bf16[256,256]{1,0:T(8,128)(2,1)S(1)} %copy-done.2, bf16[256,256]{1,0:T(8,128)(2,1)S(1)} %copy-done.3, bf16[128,256]{1,0:T(8,128)(2,1)S(1)} %copy-done.4, ...), custom_call_target="tpu_custom_call" | custom-call | flops 536870912 | bytes 1048576 | tf_op jit(solution)/shard_map/pallas_call | solution.py:148
  55.8 0.8 copy.33
  56.6 9.1 %all-to-all-start.1 = ((bf16[256,1,128]{2,1,0:T(2,128)(2,1)}), bf16[256,1,128]{2,1,0:T(2,128)(2,1)S(1)}, u32[]{:S(2)}, u32[]{:S(2)}) async-start(bf16[256,1,128]{2,1,0:T(2,128)(2,1)} %copy.33), calls=%async_computation.1 | async-start | bytes 262144 | tf_op jit(solution)/shard_map/all_to_all | solution.py:192
  65.7 4.1 %all-gather.1 = bf16[256,2,512]{2,0,1:T(8,128)(2,1)S(1)} all-gather(bf16[128,2,512]{2,0,1:T(8,128)(2,1)S(1)} %pad_maximum_fusion), channel_id=3, replica_groups=mesh['z'=4,'y'=8,'x'=4,'h'=2,'c'=2] {'c'}, dimensions={0}, use_global_device_ids=true | all-gather | bytes 786432 | tf_op jit(solution)/shard_map/all_gather | solution.py:172
  69.8 0.5 copy.35
  70.4 0.2 reshape.32
  70.6 6.7 %all-to-all-done.1 = bf16[256,1,128]{2,1,0:T(2,128)(2,1)S(1)} async-done(((bf16[256,1,128]{2,1,0:T(2,128)(2,1)}), bf16[256,1,128]{2,1,0:T(2,128)(2,1)S(1)}, u32[]{:S(2)}, u32[]{:S(2)}) %all-to-all-start.1) | async-done | bytes 65568 | tf_op jit(solution)/shard_map/all_to_all | solution.py:192
  77.2 0.0 copy-start.13
  77.3 5.1 %all-gather = bf16[512,1,128]{2,0,1:T(8,128)(2,1)S(1)} all-gather(bf16[256,1,128]{2,0,1:T(8,128)(2,1)S(1)} %copy.34), channel_id=2, replica_groups=mesh['z'=4,'y'=8,'x'=4,'h'=2,'c'=2] {'c'}, dimensions={0}, use_global_device_ids=true | all-gather | bytes 196608 | tf_op jit(solution)/shard_map/all_gather | solution.py:193
  82.4 0.3 fusion.3
  82.7 0.0 copy-start.14
  82.8 0.6 copy-done.14
  83.4 0.5 fusion.1
  83.9 0.7 copy.41
  84.6 3.6 %all-to-all-start.2 = ((bf16[4,128,128]{2,1,0:T(8,128)(2,1)}), bf16[4,128,128]{2,1,0:T(8,128)(2,1)S(1)}, u32[]{:S(2)}, u32[]{:S(2)}) async-start(bf16[4,128,128]{2,1,0:T(8,128)(2,1)} %bitcast.30), calls=%async_computation.2 | async-start | bytes 262144 | tf_op jit(solution)/shard_map/all_to_all | solution.py:204
  88.2 7.6 %all-to-all-done.2 = bf16[4,128,128]{2,1,0:T(8,128)(2,1)S(1)} async-done(((bf16[4,128,128]{2,1,0:T(8,128)(2,1)}), bf16[4,128,128]{2,1,0:T(8,128)(2,1)S(1)}, u32[]{:S(2)}, u32[]{:S(2)}) %all-to-all-start.2) | async-done | bytes 131104 | tf_op jit(solution)/shard_map/all_to_all | solution.py:204
  95.9 0.6 add_convert_fusion
  (16 shorter events, 0.2 us)
Async XLA Ops:
  0.0 82.8 %copy-start = (bf16[512,512]{1,0:T(8,128)(2,1)S(1)}, bf16[512,512]{1,0:T(8,128)(2,1)}, u32[]{:S(2)}) copy-start(bf16[512,512]{1,0:T(8,128)(2,1)} %param.26) | copy-start | bytes 1572868
  0.0 41.0 %collective-permute-start = (bf16[128,512]{1,0:T(8,128)(2,1)}, bf16[128,512]{1,0:T(8,128)(2,1)S(1)}, u32[]{:S(2)}, u32[]{:S(2)}) collective-permute-start(bf16[128,512]{1,0:T(8,128)(2,1)} %param.23), channel_id=1, source_target_pairs={{0,258},{128,386},{256,2},{384,130},{2,256},{130,384},{258,0},{386... | collective-permute-start | bytes 393224 | tf_op jit(solution)/shard_map/ppermute | solution.py:169
  24.8 0.7 copy-start.11
  25.5 1.3 %copy-start.9 = (bf16[2,128,128]{2,1,0:T(8,128)(2,1)S(1)}, bf16[2,128,128]{2,1,0:T(8,128)(2,1)}, u32[]{:S(2)}) copy-start(bf16[2,128,128]{2,1,0:T(8,128)(2,1)} %param.21) | copy-start | bytes 196612
  27.8 13.2 %copy-start.8 = (bf16[128,512]{1,0:T(8,128)(2,1)S(1)}, bf16[128,512]{1,0:T(8,128)(2,1)}, u32[]{:S(2)}) copy-start(bf16[128,512]{1,0:T(8,128)(2,1)} %param.23) | copy-start | bytes 393220
  27.8 25.5 %all-to-all-start = ((bf16[128,5,128]{2,1,0:T(8,128)(2,1)}), bf16[128,5,128]{2,1,0:T(8,128)(2,1)S(1)}, u32[]{:S(2)}, u32[]{:S(2)}) async-start(bf16[128,5,128]{2,1,0:T(8,128)(2,1)} %copy.31), calls=%async_computation | async-start | bytes 524288 | tf_op jit(solution)/shard_map/all_to_all | solution.py:184
  39.5 0.7 copy-start.10
  40.2 0.7 copy-start.12
  41.1 12.2 %copy-start.4 = (bf16[128,256]{1,0:T(8,128)(2,1)S(1)}, bf16[128,256]{1,0:T(8,128)(2,1)}, u32[]{:S(2)}) copy-start(bf16[128,256]{1,0:T(8,128)(2,1)} %constant.69.clone.back_high) | copy-start | bytes 196612
  41.1 12.2 %copy-start.5 = (bf16[128,256]{1,0:T(8,128)(2,1)S(1)}, bf16[128,256]{1,0:T(8,128)(2,1)}, u32[]{:S(2)}) copy-start(bf16[128,256]{1,0:T(8,128)(2,1)} %constant.70.clone.back_low) | copy-start | bytes 196612
  41.1 12.2 %copy-start.6 = (f32[128,128]{1,0:T(8,128)S(1)}, f32[128,128]{1,0:T(8,128)}, u32[]{:S(2)}) copy-start(f32[128,128]{1,0:T(8,128)} %constant.71.clone.turn_real) | copy-start | bytes 196612
  41.1 12.2 %copy-start.7 = (f32[128,128]{1,0:T(8,128)S(1)}, f32[128,128]{1,0:T(8,128)}, u32[]{:S(2)}) copy-start(f32[128,128]{1,0:T(8,128)} %constant.72.clone.turn_imag) | copy-start | bytes 196612
  41.2 12.2 %copy-start.1 = (bf16[256,256]{1,0:T(8,128)(2,1)S(1)}, bf16[256,256]{1,0:T(8,128)(2,1)}, u32[]{:S(2)}) copy-start(bf16[256,256]{1,0:T(8,128)(2,1)} %constant.66.clone.outer) | copy-start | bytes 393220
  41.2 12.2 %copy-start.2 = (bf16[256,256]{1,0:T(8,128)(2,1)S(1)}, bf16[256,256]{1,0:T(8,128)(2,1)}, u32[]{:S(2)}) copy-start(bf16[256,256]{1,0:T(8,128)(2,1)} %constant.67.clone.inner_high) | copy-start | bytes 393220
  41.2 12.2 %copy-start.3 = (bf16[256,256]{1,0:T(8,128)(2,1)S(1)}, bf16[256,256]{1,0:T(8,128)(2,1)}, u32[]{:S(2)}) copy-start(bf16[256,256]{1,0:T(8,128)(2,1)} %constant.68.clone.inner_low) | copy-start | bytes 393220
  56.6 20.6 %all-to-all-start.1 = ((bf16[256,1,128]{2,1,0:T(2,128)(2,1)}), bf16[256,1,128]{2,1,0:T(2,128)(2,1)S(1)}, u32[]{:S(2)}, u32[]{:S(2)}) async-start(bf16[256,1,128]{2,1,0:T(2,128)(2,1)} %copy.33), calls=%async_computation.1 | async-start | bytes 262144 | tf_op jit(solution)/shard_map/all_to_all | solution.py:192
  77.2 5.5 %copy-start.13 = (bf16[512,512]{1,0:T(8,128)(2,1)S(1)}, bf16[512,512]{1,0:T(8,128)(2,1)}, u32[]{:S(2)}) copy-start(bf16[512,512]{1,0:T(8,128)(2,1)} %param.25) | copy-start | bytes 1572868
  82.7 0.7 copy-start.14
  84.6 11.2 %all-to-all-start.2 = ((bf16[4,128,128]{2,1,0:T(8,128)(2,1)}), bf16[4,128,128]{2,1,0:T(8,128)(2,1)S(1)}, u32[]{:S(2)}, u32[]{:S(2)}) async-start(bf16[4,128,128]{2,1,0:T(8,128)(2,1)} %bitcast.30), calls=%async_computation.2 | async-start | bytes 262144 | tf_op jit(solution)/shard_map/all_to_all | solution.py:204
where the time goes:
time: 97 us; the launch traced here: 96.5 us
  starting transfers between devices  36 us (37%)
  waiting for transfers between devices  26.4 us (27%)
  blocking collectives  22.4 us (23%)
  local copies, waits for them, and re-layouts  5.89 us (6%)
  Pallas kernels  2.39 us (2%)
  matrix products  2.12 us (2%)
  other arithmetic  1.03 us (1%)
    all_gather x1, blocking collectives, local(): whole = lax.all_gather(tokens, CH, axis=1, tiled=True)  13.2 us
    all_to_all x1, waiting for transfers between devices, local(): lax.all_to_all(outgoing, SEQ, split_axis=0, concat_axis=0, tiled=True)  12.1 us
    all_to_all x1, starting transfers between devices, local(): lax.all_to_all(outgoing, SEQ, split_axis=0, concat_axis=0, tiled=True)  11.6 us
    ppermute x1, starting transfers between devices, whole_w_out(): other = lax.ppermute(w_out, ('z', 'h'), other_half_pairs())  11.6 us
    all_to_all x1, starting transfers between devices, local(): lax.all_to_all(doubled, SEQ + ('h',), split_axis=0, concat_axis=0, tiled=...  9.11 us
    all_to_all x1, waiting for transfers between devices, local(): pieces = lax.all_to_all(pieces, CH, split_axis=0, concat_axis=0, tiled=True)  7.61 us
    all_to_all x1, waiting for transfers between devices, local(): lax.all_to_all(doubled, SEQ + ('h',), split_axis=0, concat_axis=0, tiled=...  6.67 us
    all_gather x1, blocking collectives, local(): both = lax.all_gather(returned, 'c', axis=0, tiled=True)  5.15 us
  transfers between devices with their start and end apart: 4, of which 3 were waited for; matrix products, arithmetic and copies ran while one was open for 4% of the time, Pallas kernels for 0%

commit v1 on v0

v1 whole, which is shorter than its diff:
```python
import jax
import jax.numpy as jnp
import ml_dtypes
import numpy as np
from jax import lax
from jax.experimental import pallas as pl
from jax.experimental.pallas import tpu as pltpu
from jax.sharding import Mesh, PartitionSpec as P

epsilon = 1e-06

SEQ = ("z", "y", "x")
CH = ("h", "c")


def rms_norm(values, gain):
    wide = values.astype(jnp.float32)
    scale = lax.rsqrt(jnp.mean(wide * wide, axis=-1, keepdims=True) + epsilon)
    return (wide * scale * gain).astype(jnp.bfloat16)


def halves_of(table):
    high = table.astype(ml_dtypes.bfloat16)
    low = (table - high.astype(np.float64)).astype(ml_dtypes.bfloat16)
    return high, low


def transform_tables(rows, cols):
    size = rows * cols
    row = np.arange(rows, dtype=np.float64)
    col = np.arange(cols, dtype=np.float64)
    outer_angle = 2.0 * np.pi * (((row[:, None] + 0.25) * row[None, :]) % rows) / rows
    inner_angle = 2.0 * np.pi * ((col[:, None] * col[None, :]) % cols) / cols
    turn_angle = 2.0 * np.pi * (row[:, None] + 0.25) * col[None, :] / size
    outer = np.concatenate([np.cos(outer_angle), -np.sin(outer_angle)], axis=0)
    cos, sin = np.cos(inner_angle), np.sin(inner_angle)
    inner = np.block([[cos, -sin], [sin, cos]])
    outer_high, outer_low = halves_of(outer)
    inner_high, inner_low = halves_of(inner)
    back_high, back_low = halves_of(outer.T / size)
    products = [np.concatenate([outer_high, outer_low], axis=1)]
    products += [inner_high, inner_low, np.concatenate([back_high, back_low], axis=0)]
    turn = np.stack([np.cos(turn_angle), -np.sin(turn_angle)])
    return np.stack(products), turn.astype(np.float32)


def dot(left, right):
    return jnp.dot(left, right, preferred_element_type=jnp.float32)


def split(values):
    high = values.astype(jnp.bfloat16)
    return high, (values - high.astype(jnp.float32)).astype(jnp.bfloat16)


def dot_split(values, high_table, low_table):
    high, low = split(values)
    rows = values.shape[0]
    both = dot(jnp.concatenate([high, low], axis=0), high_table)
    return both[:rows] + both[rows:] + dot(high, low_table)


def delayed(values, by):
    rows, cols = values.shape
    turned = pltpu.roll(values, by, 1)
    above = pltpu.roll(turned, 1, 0)
    row = lax.broadcasted_iota(jnp.int32, (rows, cols), 0)
    col = lax.broadcasted_iota(jnp.int32, (rows, cols), 1)
    return jnp.where(col >= by, turned, jnp.where(row >= 1, above, 0.0))


def round_bf16(values):
    return values.astype(jnp.bfloat16).astype(jnp.float32)


def channel_kernel(mine, short_w, bias, u, products, turn, mixed):
    rows, cols = u.shape[1], u.shape[2]
    outer, inner_high, inner_low = products[0], products[1], products[2]
    back_high, back_low = products[3, :rows], products[3, rows:]
    turn_real, turn_imag = turn[0], turn[1]
    per_channel = jnp.concatenate([short_w[k] for k in range(short_w.shape[0])] + [bias[...]], axis=0)
    column = lax.broadcasted_iota(jnp.int32, per_channel.shape, 1)
    scalars = jnp.sum(jnp.where(column == mine[0], per_channel, 0.0), axis=1, keepdims=True)
    scalars = [scalars[k : k + 1] for k in range(scalars.shape[0])]

    def short(k):
        values = u[k].astype(jnp.float32)
        total = scalars[3 * k] * values
        total = total + scalars[3 * k + 1] * delayed(values, 1)
        total = total + scalars[3 * k + 2] * delayed(values, 2)
        return total.astype(jnp.bfloat16)

    def forward(signals):
        count = len(signals)
        side = jnp.concatenate(signals, axis=1) if count > 1 else signals[0]
        first = dot(outer, jnp.concatenate([side, side], axis=0))
        turned = []
        for k in range(count):
            real = first[:rows, k * cols : (k + 1) * cols]
            imag = first[rows:, k * cols : (k + 1) * cols]
            turned.append(
                jnp.concatenate(
                    [
                        real * turn_real - imag * turn_imag,
                        real * turn_imag + imag * turn_real,
                    ],
                    axis=1,
                )
            )
        stacked = jnp.concatenate(turned, axis=0) if count > 1 else turned[0]
        spectra = dot_split(stacked, inner_high, inner_low)
        return [
            (spectra[k * rows : (k + 1) * rows, :cols], spectra[k * rows : (k + 1) * rows, cols:])
            for k in range(count)
        ]

    def inverse(one, two):
        real = one[0] * two[0] - one[1] * two[1]
        negated = -one[0] * two[1] - one[1] * two[0]
        inner = dot_split(
            jnp.concatenate([real, negated], axis=1), inner_high, inner_low
        )
        real, negated = inner[:, :cols], inner[:, cols:]
        turned = jnp.concatenate(
            [
                real * turn_real - negated * turn_imag,
                -negated * turn_real - real * turn_imag,
            ],
            axis=0,
        )
        high, low = split(turned)
        side = dot(back_high, jnp.concatenate([high, low], axis=1))
        return side[:, :cols] + side[:, cols:] + dot(back_low, high)

    v = short(0)
    signal, response_one, response_two = forward([v, u[3], u[4]])
    first = inverse(signal, response_one) + scalars[9] * v.astype(jnp.float32)
    gated = (short(1).astype(jnp.float32) * round_bf16(first)).astype(jnp.bfloat16)
    (signal,) = forward([gated])
    second = inverse(signal, response_two) + scalars[10] * gated.astype(jnp.float32)
    mixed[...] = (short(2).astype(jnp.float32) * round_bf16(second)).astype(jnp.bfloat16)


def call(
    kernel, out_shape, flops, *operands, scalars=0, source=pltpu.VMEM, scratch=(), limit=16
):
    vmem = pl.BlockSpec(memory_space=pltpu.VMEM)
    smem = pl.BlockSpec(memory_space=pltpu.SMEM)
    held = pl.BlockSpec(memory_space=source)
    return pl.pallas_call(
        kernel,
        out_shape=out_shape,
        in_specs=[smem] * scalars + [held] * (len(operands) - scalars),
        out_specs=jax.tree.map(lambda _: vmem, out_shape),
        scratch_shapes=scratch,
        compiler_params=pltpu.CompilerParams(vmem_limit_bytes=limit * 2**20),
        cost_estimate=pl.CostEstimate(flops=flops, bytes_accessed=2**20, transcendentals=0),
    )(*operands)


def load_kernel(half, parity, *refs):
    count = (len(refs) - 2) // 2
    sources, (sent, *held), sems = refs[:count], refs[count:-1], refs[-1]
    w_up, w_out, w_down = sources[:3]
    units, wide = w_up.shape
    rows = w_out.shape[0]
    part = wide // 2
    there = pl.ds(pl.multiple_of((1 - half[0]) * part, part), part)
    here = pl.ds(pl.multiple_of(half[0] * part, part), part)
    turn = pl.ds(pl.multiple_of(parity[0] * part, part), part)
    pairs = [
        (w_up.at[:, turn], sent.at[pl.ds(0, units)]),
        (w_down.at[turn, there], sent.at[pl.ds(units, part)]),
        (w_out.at[:, pl.ds(0, part)], sent.at[pl.ds(units + part, rows)]),
        (w_out.at[:, pl.ds(part, part)], sent.at[pl.ds(units + part + rows, rows)]),
        (w_down.at[:, here], held[0]),
        (w_up, held[1]),
        (w_out, held[2]),
    ]
    pairs += list(zip(sources[3:], held[3:]))
    copies = [
        pltpu.make_async_copy(source, target, sems.at[k])
        for k, (source, target) in enumerate(pairs)
    ]
    for copy in copies:
        copy.start()
    for copy in copies:
        copy.wait()


def load(half, parity, w_up, w_out, w_down, *arrays):
    sources = [w_up, w_out, w_down, *arrays]
    sources = [pltpu.with_memory_space_constraint(array, pltpu.HBM) for array in sources]
    units, wide = w_up.shape
    part = wide // 2
    held = [
        pltpu.VMEM((units + part + 2 * w_out.shape[0], part), w_up.dtype),
        pltpu.VMEM((units, part), w_down.dtype),
    ]
    held += [pltpu.VMEM(array.shape, array.dtype) for array in (w_up, w_out, *arrays)]
    sems = [pltpu.SemaphoreType.DMA((len(sources) + 4,))]
    return call(
        load_kernel, held, 0, half, parity, *sources, source=pltpu.HBM, scratch=sems, scalars=2
    )


def project_kernel(whole, gain, w_in, filters, outgoing):
    normed = rms_norm(whole[...], gain[...])
    count = w_in.shape[0]
    for k in range(count):
        outgoing[k] = lax.dot_general(
            w_in[k], normed, (((0,), (1,)), ((), ())), preferred_element_type=jnp.float32
        ).astype(jnp.bfloat16)
    for k in range(filters.shape[0]):
        outgoing[count + k] = filters[k]


def out_kernel(half, arrived, own, near, partial):
    rows = arrived.shape[1]
    first = near.shape[0] - 2 * rows
    other = jnp.concatenate([near[first : first + rows], near[first + rows :]], axis=1)
    low = half[0] == 0
    weights = (jnp.where(low, own[...], other), jnp.where(low, other, own[...]))
    parts = [
        lax.dot_general(
            arrived[k], weights[k], (((0,), (0,)), ((), ())), preferred_element_type=jnp.float32
        )
        for k in range(2)
    ]
    partial[...] = parts[0] + parts[1]


def mlp_kernel(place, parity, whole, shares, gain, w_up, w_down, near, far, pieces, own):
    count, _, width = pieces.shape
    units = whole.shape[1]
    half_units = units // 2
    share = shares[0] + shares[1]
    middle = (whole[...].astype(jnp.float32) + share).astype(jnp.bfloat16)
    mine = middle[:, :width]
    for k in range(1, units // width):
        mine = jnp.where(place[0] == k, middle[:, k * width : (k + 1) * width], mine)
    own[...] = mine
    normed = rms_norm(middle, gain[...])
    hidden = jax.nn.gelu(dot(normed, w_up[...])).astype(jnp.bfloat16)
    partial = dot(hidden, w_down[...])
    for part in (near, far):
        hidden = jax.nn.gelu(dot(normed, part[:units])).astype(jnp.bfloat16)
        partial = partial + dot(hidden, part[units : units + half_units])
    partial = partial.astype(jnp.bfloat16)
    for k in range(count):
        pieces[k] = partial[:, k * width : (k + 1) * width]


def other_half_pairs():
    pairs = []
    for z in range(8):
        there = (z + 2) % 8
        if there // 4 == z // 4:
            there = (z - 2) % 8
        pairs.append((z % 4 * 2 + z // 4, there % 4 * 2 + there // 4))
    return pairs


def local(tokens, gain_mix, w_in, short_w, filters, conv_bias, w_out, gain_mlp, w_up, w_down):
    samples, width = tokens.shape
    shards = lax.axis_size(SEQ)
    blocks = lax.axis_size(CH)
    shape = jax.ShapeDtypeStruct
    mine = lax.axis_index(SEQ).astype(jnp.int32)[None]
    place = lax.axis_index(CH).astype(jnp.int32)[None]
    half = lax.axis_index("h").astype(jnp.int32)[None]
    parity = (lax.axis_index("x") % 2).astype(jnp.int32)[None]
    tables = [jnp.asarray(table) for table in transform_tables(shards, samples)]
    (
        sent,
        w_down,
        w_up,
        w_out,
        tokens,
        gain_mix,
        w_in,
        short_w,
        filters,
        conv_bias,
        gain_mlp,
        *tables,
    ) = load(
        half,
        parity,
        w_up,
        w_out,
        w_down,
        tokens,
        gain_mix[None],
        w_in,
        short_w,
        filters,
        conv_bias,
        gain_mlp[None],
        *tables,
    )
    whole = lax.all_gather(tokens, CH, axis=1, tiled=True)
    outgoing = call(
        project_kernel,
        shape((5, width, samples), jnp.bfloat16),
        2**26,
        whole,
        gain_mix,
        w_in,
        filters,
    )
    outgoing, sent, half, parity, place, mine = lax.optimization_barrier(
        (outgoing.transpose(1, 0, 2), sent, half, parity, place, mine)
    )
    arrived = lax.all_to_all(outgoing, SEQ, split_axis=0, concat_axis=0, tiled=True)
    near = lax.ppermute(sent, ("z", "h"), other_half_pairs())
    far = lax.ppermute(near[: width * blocks * 3 // 2], "x", [(k, k ^ 1) for k in range(lax.axis_size("x"))])
    mixed = call(
        channel_kernel,
        shape((shards, samples), jnp.bfloat16),
        2**29,
        mine,
        short_w,
        conv_bias,
        arrived.transpose(1, 0, 2),
        *tables,
        scalars=1,
    )
    doubled = jnp.concatenate([mixed, mixed], axis=0)
    returned = lax.all_to_all(doubled, ("h",) + SEQ, split_axis=0, concat_axis=0, tiled=True)
    partial = call(
        out_kernel,
        shape((samples, blocks * width), jnp.float32),
        2**31,
        half,
        returned.reshape(2, shards, samples),
        w_out,
        near,
        scalars=1,
    )
    shares = lax.all_gather(partial, "c", axis=0)
    pieces, own = call(
        mlp_kernel,
        (shape((2, samples, width), jnp.bfloat16), shape((samples, width), jnp.bfloat16)),
        2**28,
        place,
        parity,
        whole,
        shares,
        gain_mlp,
        w_up,
        w_down,
        near,
        far,
        scalars=2,
    )
    pieces = lax.all_gather(pieces, "c", axis=0)
    pieces = lax.dynamic_index_in_dim(pieces, place[0] % 2, 1, keepdims=False)
    total = jnp.sum(pieces.astype(jnp.float32), axis=0)
    return (own.astype(jnp.float32) + total).astype(jnp.bfloat16)


def solution(mesh):
    fine = Mesh(mesh.devices.reshape(4, 8, 4, 2, 2), SEQ + CH)
    return jax.shard_map(
        local,
        mesh=fine,
        in_specs=(
            P(SEQ, CH),
            P(),
            P(None, None, CH),
            P(None, None, CH),
            P(None, CH, SEQ),
            P(None, CH),
            P(CH, None),
            P(),
            P(None, CH),
            P(CH, None),
        ),
        out_specs=P(SEQ, CH),
        check_vma=False,
    )
```

time: 97 us -> 82.2 us (0.85)
  waiting for transfers between devices: 26.4 us -> 17 us
  local copies, waits for them, and re-layouts: 5.89 us -> 1.63 us
  Pallas kernels: 2.39 us -> 5 us
  matrix products: 2.12 us -> 0 us
  starting transfers between devices: 36 us -> 35 us
    all_to_all x1, waiting for transfers between devices: 12.1 us -> 7.03 us  [local(): lax.all_to_all(outgoing, SEQ, split_axis=0, concat_axis=0, tiled=True)]
    all_to_all x2 -> x1, waiting for transfers between devices: 14.3 us -> 9.96 us  [local(): lax.all_to_all(doubled, ('h',) + SEQ, split_axis=0, concat_axis=0, tiled=...]
    all_gather x1, blocking collectives: 13.2 us -> 16.1 us  [local(): whole = lax.all_gather(tokens, CH, axis=1, tiled=True)]
    all_gather x2, blocking collectives: 9.26 us -> 6.42 us  [the longest x1 4.5 us: local(): shares = lax.all_gather(partial, 'c', axis=0)]
    unnamed x31 -> x1, local copies, waits for them, and re-layouts: 2.76 us -> 0.01 us
    pallas_call x1 -> x5, Pallas kernels: 2.39 us -> 5 us  [call(): pl.pallas_call(kernel, out_shape=out_shape, in_specs=[smem] * scalars + [...]
    ppermute x1 -> x2, starting transfers between devices: 11.6 us -> 9.03 us  [the longest x1 7.11 us: local(): near = lax.ppermute(sent, ('z', 'h'), other_half_pairs())]
    dot_general x3 -> x0, matrix products: 2.12 us -> none  [the longest x1 1.3 us: local(): jnp.einsum('td,kde->ekt', normed, w_in, preferred_element_type=jnp.float32)]
  transfers between devices with their start and end apart: 4 -> 4, of which waited for: 3 -> 2; matrix products, arithmetic and copies ran while one was open for 4% -> 1% of each run, Pallas kernels for 0% -> 3%
where the time goes in v1:
time: 82.2 us; the launch traced here: 81.9 us
  starting transfers between devices  35 us (43%)
  blocking collectives  22.5 us (27%)
  waiting for transfers between devices  17 us (21%)
  Pallas kernels  5 us (6%)
  local copies, waits for them, and re-layouts  1.63 us (2%)
    all_gather x1, blocking collectives, local(): whole = lax.all_gather(tokens, CH, axis=1, tiled=True)  16.1 us
    all_to_all x1, starting transfers between devices, local(): lax.all_to_all(doubled, ('h',) + SEQ, split_axis=0, concat_axis=0, tiled=...  13.8 us
    all_to_all x1, starting transfers between devices, local(): lax.all_to_all(outgoing, SEQ, split_axis=0, concat_axis=0, tiled=True)  12.1 us
    all_to_all x1, waiting for transfers between devices, local(): lax.all_to_all(doubled, ('h',) + SEQ, split_axis=0, concat_axis=0, tiled=...  9.96 us
    ppermute x1, starting transfers between devices, local(): near = lax.ppermute(sent, ('z', 'h'), other_half_pairs())  7.11 us
    all_to_all x1, waiting for transfers between devices, local(): lax.all_to_all(outgoing, SEQ, split_axis=0, concat_axis=0, tiled=True)  7.03 us
    pallas_call x5, Pallas kernels, call(): pl.pallas_call(kernel, out_shape=out_shape, in_specs=[smem] * scalars + [...  5 us
    all_gather x1, blocking collectives, local(): shares = lax.all_gather(partial, 'c', axis=0)  4.5 us
  transfers between devices with their start and end apart: 4, of which 2 were waited for; matrix products, arithmetic and copies ran while one was open for 1% of the time, Pallas kernels for 3%

profile of v1, /device:TPU:1, one launch (start us, length us, event | category | flops | bytes accessed | tf_op | source)
XLA Modules:
  0.0 81.9 jit_solution(5008723150704517810)
XLA Ops:
  0.0 1.8 %shard_map.118 = (bf16[1024,256]{1,0:T(8,128)(2,1)S(1)}, bf16[512,256]{1,0:T(8,128)(2,1)S(1)}, bf16[512,512]{1,0:T(8,128)(2,1)S(1)}, bf16[128,512]{1,0:T(8,128)(...) custom-call(s32[1]{0:T(128)} %bitcast.half, ...), custom_call_target="tpu_custom_call" | custom-call | bytes 1048576 | tf_op jit(solution)/shard_map/pallas_call | solution.py:150
  1.9 16.1 %all_gather.15.whole = bf16[128,512]{1,0:T(8,128)(2,1)S(1)} all-gather(bf16[128,128]{1,0:T(8,128)(2,1)S(1)} %get-tuple-element.26), channel_id=1, replica_groups=mesh['z'=4,'y'=8,'x'=4,'h'=2,'c'=2] {'h','c'}, dimensions={1}, use_global_device_ids=true | all-gather | bytes 163840 | tf_op jit(solution)/shard_map/all_gather | solution.py:302
  17.9 0.4 shard_map.119
  18.3 0.8 %copy.16 = bf16[128,5,128]{2,1,0:T(8,128)(2,1)} copy(bf16[128,5,128]{2,0,1:T(8,128)(2,1)S(1)} %bitcast.17) | data formatting | bytes 327680 | tf_op jit(solution)/shard_map/optimization_barrier | solution.py:312
  19.1 12.1 %all-to-all-start = ((bf16[128,5,128]{2,1,0:T(8,128)(2,1)}), bf16[128,5,128]{2,1,0:T(8,128)(2,1)S(1)}, u32[]{:S(2)}, u32[]{:S(2)}) async-start(bf16[128,5,128]{2,1,0:T(8,128)(2,1)} %copy.16), calls=%async_computation | async-start | bytes 524288 | tf_op jit(solution)/shard_map/all_to_all | solution.py:315
  31.2 7.1 %collective-permute-start = (bf16[1024,256]{1,0:T(8,128)(2,1)S(1)}, bf16[1024,256]{1,0:T(8,128)(2,1)S(1)}, u32[]{:S(2)}, u32[]{:S(2)}) collective-permute-start(bf16[1024,256]{1,0:T(8,128)(2,1)S(1)} %get-tuple-element.41), channel_id=1, source_target_pairs={{0,258},{128,386},{256,2},{384,130},{2,256},{130,384},{258,0},{386... | collective-permute-start | bytes 1572872 | tf_op jit(solution)/shard_map/ppermute | solution.py:316
  38.3 7.0 %all-to-all-done = bf16[128,5,128]{2,1,0:T(8,128)(2,1)S(1)} async-done(((bf16[128,5,128]{2,1,0:T(8,128)(2,1)}), bf16[128,5,128]{2,1,0:T(8,128)(2,1)S(1)}, u32[]{:S(2)}, u32[]{:S(2)}) %all-to-all-start) | async-done | bytes 163872 | tf_op jit(solution)/shard_map/all_to_all | solution.py:315
  45.4 1.9 %shard_map.120 = bf16[128,128]{1,0:T(8,128)(2,1)S(1)} custom-call(s32[1]{0:T(128)} %bitcast.6.mine, f32[3,3,128]{2,1,0:T(4,128)S(1)} %get-tuple-element.35.short_w, f32[2,128]{1,0:T(2,128)S(1)} %get-tuple-element.36.bias, bf16[5,128,128]{2,1,0:T(8,128)(2,1)S(1)} %bitcast.18, bf16[4,256,256]{2,1,0:T(8,128)(2,1)S(1)} %get-tuple-element.38.products, ...), custom_call_target="tpu_custom_call" | custom-call | flops 536870912 | bytes 1048576 | tf_op jit(solution)/shard_map/pallas_call | solution.py:150
  47.3 0.7 copy.18
  48.0 13.8 %all-to-all-start.1 = ((bf16[256,1,128]{2,1,0:T(2,128)(2,1)}), bf16[256,1,128]{2,1,0:T(2,128)(2,1)S(1)}, u32[]{:S(2)}, u32[]{:S(2)}) async-start(bf16[256,1,128]{2,1,0:T(2,128)(2,1)} %copy.18), calls=%async_computation.1 | async-start | bytes 262144 | tf_op jit(solution)/shard_map/all_to_all | solution.py:330
  61.9 0.0 collective-permute-done.near
  61.9 1.9 %collective-permute-start.1 = (bf16[768,256]{1,0:T(8,128)(2,1)S(1)}, bf16[768,256]{1,0:T(8,128)(2,1)S(1)}, u32[]{:S(2)}, u32[]{:S(2)}) collective-permute-start(bf16[768,256]{1,0:T(8,128)(2,1)S(1)} %slice.4), channel_id=1, source_target_pairs={{0,4},{4,0},{8,12},{12,8},{1,5},{5,1},{9,13},{13,9},{2,6},{6,2},{1... | collective-permute-start | bytes 1179656 | tf_op jit(solution)/shard_map/ppermute | solution.py:317
  63.9 10.0 %all-to-all-done.1 = bf16[256,1,128]{2,1,0:T(2,128)(2,1)S(1)} async-done(((bf16[256,1,128]{2,1,0:T(2,128)(2,1)}), bf16[256,1,128]{2,1,0:T(2,128)(2,1)S(1)}, u32[]{:S(2)}, u32[]{:S(2)}) %all-to-all-start.1) | async-done | bytes 65568 | tf_op jit(solution)/shard_map/all_to_all | solution.py:330
  73.9 0.3 shard_map.121
  74.1 4.5 %all-gather = f32[256,512]{1,0:T(8,128)S(1)} all-gather(f32[128,512]{1,0:T(8,128)S(1)} %shard_map.121), channel_id=2, replica_groups=mesh['z'=4,'y'=8,'x'=4,'h'=2,'c'=2] {'c'}, dimensions={0}, use_global_device_ids=true | all-gather | bytes 786432 | tf_op jit(solution)/shard_map/all_gather | solution.py:341
  78.6 0.0 collective-permute-done.1.far
  78.6 0.7 shard_map.122
  79.3 1.9 %all-gather.1 = bf16[4,128,128]{2,1,0:T(8,128)(2,1)S(1)} all-gather(bf16[2,128,128]{2,1,0:T(8,128)(2,1)S(1)} %get-tuple-element.46), channel_id=3, replica_groups=mesh['z'=4,'y'=8,'x'=4,'h'=2,'c'=2] {'c'}, dimensions={0}, use_global_device_ids=true | all-gather | bytes 196608 | tf_op jit(solution)/shard_map/all_gather | solution.py:357
  81.2 0.6 add_convert_fusion
  (5 shorter events, 0.1 us)
Async XLA Ops:
  19.1 26.3 %all-to-all-start = ((bf16[128,5,128]{2,1,0:T(8,128)(2,1)}), bf16[128,5,128]{2,1,0:T(8,128)(2,1)S(1)}, u32[]{:S(2)}, u32[]{:S(2)}) async-start(bf16[128,5,128]{2,1,0:T(8,128)(2,1)} %copy.16), calls=%async_computation | async-start | bytes 524288 | tf_op jit(solution)/shard_map/all_to_all | solution.py:315
  31.2 30.7 %collective-permute-start = (bf16[1024,256]{1,0:T(8,128)(2,1)S(1)}, bf16[1024,256]{1,0:T(8,128)(2,1)S(1)}, u32[]{:S(2)}, u32[]{:S(2)}) collective-permute-start(bf16[1024,256]{1,0:T(8,128)(2,1)S(1)} %get-tuple-element.41), channel_id=1, source_target_pairs={{0,258},{128,386},{256,2},{384,130},{2,256},{130,384},{258,0},{386... | collective-permute-start | bytes 1572872 | tf_op jit(solution)/shard_map/ppermute | solution.py:316
  48.0 25.8 %all-to-all-start.1 = ((bf16[256,1,128]{2,1,0:T(2,128)(2,1)}), bf16[256,1,128]{2,1,0:T(2,128)(2,1)S(1)}, u32[]{:S(2)}, u32[]{:S(2)}) async-start(bf16[256,1,128]{2,1,0:T(2,128)(2,1)} %copy.18), calls=%async_computation.1 | async-start | bytes 262144 | tf_op jit(solution)/shard_map/all_to_all | solution.py:330
  61.9 16.7 %collective-permute-start.1 = (bf16[768,256]{1,0:T(8,128)(2,1)S(1)}, bf16[768,256]{1,0:T(8,128)(2,1)S(1)}, u32[]{:S(2)}, u32[]{:S(2)}) collective-permute-start(bf16[768,256]{1,0:T(8,128)(2,1)S(1)} %slice.4), channel_id=1, source_target_pairs={{0,4},{4,0},{8,12},{12,8},{1,5},{5,1},{9,13},{13,9},{2,6},{6,2},{1... | collective-permute-start | bytes 1179656 | tf_op jit(solution)/shard_map/ppermute | solution.py:317

commit v2 on v1

--- a/solution.py
+++ b/solution.py
@@ -11,6 +11,7 @@
 
 SEQ = ("z", "y", "x")
 CH = ("h", "c")
+DEEP, HIGH, WIDE = 4, 8, 4
 
 
 def rms_norm(values, gain):
@@ -25,8 +26,33 @@
     return high, low
 
 
-def transform_tables(rows, cols):
+def first_ranks(deep, high, wide):
+    return [
+        ((deep - 1 - z) * high + (y + high // 2) % high) * wide + (x + wide // 2) % wide
+        for z in range(deep)
+        for y in range(high)
+        for x in range(wide)
+    ]
+
+
+def second_ranks(deep, high, wide):
+    return [
+        (((1 - h) * deep + z) * high + (y + high // 2) % high) * wide + (x + wide // 2) % wide
+        for h in range(2)
+        for z in range(deep)
+        for y in range(high)
+        for x in range(wide)
+    ]
+
+
+def previous_rows(times):
+    times = np.asarray(times)
+    return (times[:, None] == times[None, :] + 1).astype(ml_dtypes.bfloat16)
+
+
+def transform_tables(rows, cols, times):
     size = rows * cols
+    times = np.asarray(times)
     row = np.arange(rows, dtype=np.float64)
     col = np.arange(cols, dtype=np.float64)
     outer_angle = 2.0 * np.pi * (((row[:, None] + 0.25) * row[None, :]) % rows) / rows
@@ -35,6 +61,7 @@
     outer = np.concatenate([np.cos(outer_angle), -np.sin(outer_angle)], axis=0)
     cos, sin = np.cos(inner_angle), np.sin(inner_angle)
     inner = np.block([[cos, -sin], [sin, cos]])
+    outer = outer[:, times]
     outer_high, outer_low = halves_of(outer)
     inner_high, inner_low = halves_of(inner)
     back_high, back_low = halves_of(outer.T / size)
@@ -60,21 +87,23 @@
     return both[:rows] + both[rows:] + dot(high, low_table)
 
 
-def delayed(values, by):
-    rows, cols = values.shape
-    turned = pltpu.roll(values, by, 1)
-    above = pltpu.roll(turned, 1, 0)
-    row = lax.broadcasted_iota(jnp.int32, (rows, cols), 0)
-    col = lax.broadcasted_iota(jnp.int32, (rows, cols), 1)
-    return jnp.where(col >= by, turned, jnp.where(row >= 1, above, 0.0))
+def delayed(values, above, by):
+    col = lax.broadcasted_iota(jnp.int32, values.shape, 1)
+    return jnp.where(col >= by, pltpu.roll(values, by, 1), pltpu.roll(above, by, 1))
+
+
+def turned_blocks(values):
+    step = values.shape[0] // DEEP
+    return [values[k * step : (k + 1) * step] for k in reversed(range(DEEP))]
 
 
 def round_bf16(values):
     return values.astype(jnp.bfloat16).astype(jnp.float32)
 
 
-def channel_kernel(mine, short_w, bias, u, products, turn, mixed):
+def channel_kernel(mine, short_w, bias, u, previous, products, turn, mixed):
     rows, cols = u.shape[1], u.shape[2]
+    above = dot(previous[...], jnp.concatenate([u[0], u[1], u[2]], axis=1))
     outer, inner_high, inner_low = products[0], products[1], products[2]
     back_high, back_low = products[3, :rows], products[3, rows:]
     turn_real, turn_imag = turn[0], turn[1]
@@ -86,8 +115,9 @@
     def short(k):
         values = u[k].astype(jnp.float32)
         total = scalars[3 * k] * values
-        total = total + scalars[3 * k + 1] * delayed(values, 1)
-        total = total + scalars[3 * k + 2] * delayed(values, 2)
+        past = above[:, k * cols : (k + 1) * cols]
+        total = total + scalars[3 * k + 1] * delayed(values, past, 1)
+        total = total + scalars[3 * k + 2] * delayed(values, past, 2)
         return total.astype(jnp.bfloat16)
 
     def forward(signals):
@@ -138,7 +168,8 @@
     gated = (short(1).astype(jnp.float32) * round_bf16(first)).astype(jnp.bfloat16)
     (signal,) = forward([gated])
     second = inverse(signal, response_two) + scalars[10] * gated.astype(jnp.float32)
-    mixed[...] = (short(2).astype(jnp.float32) * round_bf16(second)).astype(jnp.bfloat16)
+    product = (short(2).astype(jnp.float32) * round_bf16(second)).astype(jnp.bfloat16)
+    mixed[...] = jnp.concatenate(turned_blocks(product), axis=0)
 
 
 def call(
@@ -158,26 +189,7 @@
     )(*operands)
 
 
-def load_kernel(half, parity, *refs):
-    count = (len(refs) - 2) // 2
-    sources, (sent, *held), sems = refs[:count], refs[count:-1], refs[-1]
-    w_up, w_out, w_down = sources[:3]
-    units, wide = w_up.shape
-    rows = w_out.shape[0]
-    part = wide // 2
-    there = pl.ds(pl.multiple_of((1 - half[0]) * part, part), part)
-    here = pl.ds(pl.multiple_of(half[0] * part, part), part)
-    turn = pl.ds(pl.multiple_of(parity[0] * part, part), part)
-    pairs = [
-        (w_up.at[:, turn], sent.at[pl.ds(0, units)]),
-        (w_down.at[turn, there], sent.at[pl.ds(units, part)]),
-        (w_out.at[:, pl.ds(0, part)], sent.at[pl.ds(units + part, rows)]),
-        (w_out.at[:, pl.ds(part, part)], sent.at[pl.ds(units + part + rows, rows)]),
-        (w_down.at[:, here], held[0]),
-        (w_up, held[1]),
-        (w_out, held[2]),
-    ]
-    pairs += list(zip(sources[3:], held[3:]))
+def copy_all(pairs, sems):
     copies = [
         pltpu.make_async_copy(source, target, sems.at[k])
         for k, (source, target) in enumerate(pairs)
@@ -188,19 +200,46 @@
         copy.wait()
 
 
-def load(half, parity, w_up, w_out, w_down, *arrays):
-    sources = [w_up, w_out, w_down, *arrays]
-    sources = [pltpu.with_memory_space_constraint(array, pltpu.HBM) for array in sources]
+def first_load_kernel(half, parity, *refs):
+    count = (len(refs) + 1) // 2
+    sources, (sent, *held), sems = refs[:count], refs[count:-1], refs[-1]
+    w_up, w_down, w_out = sources[:3]
     units, wide = w_up.shape
+    rows = w_out.shape[0]
     part = wide // 2
-    held = [
-        pltpu.VMEM((units + part + 2 * w_out.shape[0], part), w_up.dtype),
-        pltpu.VMEM((units, part), w_down.dtype),
+    there = pl.ds(pl.multiple_of((1 - half[0]) * part, part), part)
+    turn = pl.ds(pl.multiple_of(parity[0] * part, part), part)
+    pairs = [
+        (w_up.at[:, turn], sent.at[pl.ds(0, units)]),
+        (w_down.at[turn, there], sent.at[pl.ds(units, part)]),
+        (w_out.at[:, pl.ds(0, part)], sent.at[pl.ds(units + part, rows)]),
+        (w_out.at[:, pl.ds(part, part)], sent.at[pl.ds(units + part + rows, rows)]),
     ]
-    held += [pltpu.VMEM(array.shape, array.dtype) for array in (w_up, w_out, *arrays)]
-    sems = [pltpu.SemaphoreType.DMA((len(sources) + 4,))]
+    copy_all(pairs + list(zip(sources[3:], held)), sems)
+
+
+def last_load_kernel(half, w_down, *refs):
+    count = (len(refs) - 2) // 2
+    sources, (down, *held), sems = refs[:count], refs[count:-1], refs[-1]
+    part = down.shape[1]
+    here = pl.ds(pl.multiple_of(half[0] * part, part), part)
+    copy_all([(w_down.at[:, here], down)] + list(zip(sources, held)), sems)
+
+
+def load(kernel, copies, cut, scalars, *arrays):
+    arrays = [pltpu.with_memory_space_constraint(array, pltpu.HBM) for array in arrays]
+    held = [pltpu.VMEM(cut, jnp.bfloat16)]
+    held += [pltpu.VMEM(array.shape, array.dtype) for array in arrays[-(copies - 1) :]]
+    sems = [pltpu.SemaphoreType.DMA((len(arrays) + 1,))]
     return call(
-        load_kernel, held, 0, half, parity, *sources, source=pltpu.HBM, scratch=sems, scalars=2
+        kernel,
+        held,
+        0,
+        *scalars,
+        *arrays,
+        scalars=len(scalars),
+        source=pltpu.HBM,
+        scratch=sems,
     )
 
 
@@ -223,7 +262,10 @@
     weights = (jnp.where(low, own[...], other), jnp.where(low, other, own[...]))
     parts = [
         lax.dot_general(
-            arrived[k], weights[k], (((0,), (0,)), ((), ())), preferred_element_type=jnp.float32
+            jnp.concatenate(turned_blocks(arrived[1 - k]), axis=0),
+            weights[k],
+            (((0,), (0,)), ((), ())),
+            preferred_element_type=jnp.float32,
         )
         for k in range(2)
     ]
@@ -261,43 +303,45 @@
     return pairs
 
 
+def neighbour_pairs():
+    high, wide = lax.axis_size("y"), lax.axis_size("x")
+    pairs = []
+    for y in range(high):
+        for x in range(wide):
+            pairs.append(((y * wide + x) * 2, (y * wide + (x ^ 1)) * 2))
+            pairs.append(((y * wide + x) * 2 + 1, ((y ^ 1) * wide + x) * 2 + 1))
+    return pairs
+
+
 def local(tokens, gain_mix, w_in, short_w, filters, conv_bias, w_out, gain_mlp, w_up, w_down):
     samples, width = tokens.shape
     shards = lax.axis_size(SEQ)
     blocks = lax.axis_size(CH)
     shape = jax.ShapeDtypeStruct
-    mine = lax.axis_index(SEQ).astype(jnp.int32)[None]
+    place_z, place_y, place_x = (lax.axis_index(axis) for axis in SEQ)
+    mine = (DEEP - 1 - place_z) * HIGH + (place_y + HIGH // 2) % HIGH
+    mine = (mine * WIDE + (place_x + WIDE // 2) % WIDE).astype(jnp.int32)[None]
+    ranks = first_ranks(DEEP, HIGH, WIDE)
     place = lax.axis_index(CH).astype(jnp.int32)[None]
     half = lax.axis_index("h").astype(jnp.int32)[None]
-    parity = (lax.axis_index("x") % 2).astype(jnp.int32)[None]
-    tables = [jnp.asarray(table) for table in transform_tables(shards, samples)]
-    (
-        sent,
+    side = jnp.where(lax.axis_index("c") == 0, lax.axis_index("x"), lax.axis_index("y"))
+    parity = (side % 2).astype(jnp.int32)[None]
+    tables = [previous_rows(ranks), *transform_tables(shards, samples, ranks)]
+    tables = [jnp.asarray(table) for table in tables]
+    units, wide = w_up.shape
+    part = wide // 2
+    sent, tokens, gain_mix, w_in, filters = load(
+        first_load_kernel,
+        5,
+        (units + part + 2 * width, part),
+        (half, parity),
+        w_up,
         w_down,
-        w_up,
         w_out,
-        tokens,
-        gain_mix,
-        w_in,
-        short_w,
-        filters,
-        conv_bias,
-        gain_mlp,
-        *tables,
-    ) = load(
-        half,
-        parity,
-        w_up,
-        w_out,
-        w_down,
         tokens,
         gain_mix[None],
         w_in,
-        short_w,
         filters,
-        conv_bias,
-        gain_mlp[None],
-        *tables,
     )
     whole = lax.all_gather(tokens, CH, axis=1, tiled=True)
     outgoing = call(
@@ -309,12 +353,27 @@
         w_in,
         filters,
     )
-    outgoing, sent, half, parity, place, mine = lax.optimization_barrier(
-        (outgoing.transpose(1, 0, 2), sent, half, parity, place, mine)
-    )
-    arrived = lax.all_to_all(outgoing, SEQ, split_axis=0, concat_axis=0, tiled=True)
+    outgoing, sent, half, parity, place, mine, w_up = lax.optimization_barrier(
+        (outgoing.transpose(1, 0, 2), sent, half, parity, place, mine, w_up)
+    )
+    arrived = lax.all_to_all(
+        outgoing, SEQ, split_axis=0, concat_axis=0, tiled=True, axis_index_groups=[ranks]
+    )
+    w_down, w_up, w_out, short_w, conv_bias, gain_mlp, *tables = load(
+        last_load_kernel,
+        9,
+        (units, part),
+        (half,),
+        w_down,
+        w_up,
+        w_out,
+        short_w,
+        conv_bias,
+        gain_mlp[None],
+        *tables,
+    )
     near = lax.ppermute(sent, ("z", "h"), other_half_pairs())
-    far = lax.ppermute(near[: width * blocks * 3 // 2], "x", [(k, k ^ 1) for k in range(lax.axis_size("x"))])
+    far = lax.ppermute(near[: width * blocks * 3 // 2], ("y", "x", "c"), neighbour_pairs())
     mixed = call(
         channel_kernel,
         shape((shards, samples), jnp.bfloat16),
@@ -327,7 +386,14 @@
         scalars=1,
     )
     doubled = jnp.concatenate([mixed, mixed], axis=0)
-    returned = lax.all_to_all(doubled, ("h",) + SEQ, split_axis=0, concat_axis=0, tiled=True)
+    returned = lax.all_to_all(
+        doubled,
+        ("h",) + SEQ,
+        split_axis=0,
+        concat_axis=0,
+        tiled=True,
+        axis_index_groups=[second_ranks(DEEP, HIGH, WIDE)],
+    )
     partial = call(
         out_kernel,
         shape((samples, blocks * width), jnp.float32),

time: 82.2 us -> 77.5 us (0.943)
  waiting for transfers between devices: 17 us -> 1.93 us
  starting transfers between devices: 35 us -> 42.4 us
  blocking collectives: 22.5 us -> 24.3 us
  Pallas kernels: 5 us -> 6.08 us
    all_to_all x1, waiting for transfers between devices: 9.96 us -> 1.39 us  [local(): lax.all_to_all(doubled, ('h',) + SEQ, split_axis=0, concat_axis=0, tiled=...]
    all_to_all x1, waiting for transfers between devices: 7.03 us -> 0.01 us  [local(): lax.all_to_all(outgoing, SEQ, split_axis=0, concat_axis=0, tiled=True, ax...]
    all_to_all x1, starting transfers between devices: 13.8 us -> 20.4 us  [local(): lax.all_to_all(doubled, ('h',) + SEQ, split_axis=0, concat_axis=0, tiled=...]
    all_to_all x1, starting transfers between devices: 12.1 us -> 14.5 us  [local(): lax.all_to_all(outgoing, SEQ, split_axis=0, concat_axis=0, tiled=True, ax...]
    all_gather x1, blocking collectives: 1.92 us -> 3.89 us  [local(): pieces = lax.all_gather(pieces, 'c', axis=0)]
    ppermute x1, starting transfers between devices: 7.11 us -> 5.17 us  [local(): near = lax.ppermute(sent, ('z', 'h'), other_half_pairs())]
    pallas_call x5 -> x6, Pallas kernels: 5 us -> 6.08 us  [call(): pl.pallas_call(kernel, out_shape=out_shape, in_specs=[smem] * scalars + [...]
  transfers between devices with their start and end apart: 4 -> 4, of which waited for: 2 -> 2; matrix products, arithmetic and copies ran while one was open for 1% -> 1% of each run, Pallas kernels for 3% -> 5%
where the time goes in v2:
time: 77.5 us; the launch traced here: 77.1 us
  starting transfers between devices  42.4 us (55%)
  blocking collectives  24.3 us (31%)
  Pallas kernels  6.08 us (8%)
  waiting for transfers between devices  1.93 us (2%)
  local copies, waits for them, and re-layouts  1.64 us (2%)
    all_to_all x1, starting transfers between devices, local(): lax.all_to_all(doubled, ('h',) + SEQ, split_axis=0, concat_axis=0, tiled=...  20.4 us
    all_gather x1, blocking collectives, local(): whole = lax.all_gather(tokens, CH, axis=1, tiled=True)  16.1 us
    all_to_all x1, starting transfers between devices, local(): lax.all_to_all(outgoing, SEQ, split_axis=0, concat_axis=0, tiled=True, ax...  14.5 us
    pallas_call x6, Pallas kernels, call(): pl.pallas_call(kernel, out_shape=out_shape, in_specs=[smem] * scalars + [...  6.08 us
    ppermute x1, starting transfers between devices, local(): near = lax.ppermute(sent, ('z', 'h'), other_half_pairs())  5.17 us
    all_gather x1, blocking collectives, local(): shares = lax.all_gather(partial, 'c', axis=0)  4.38 us
    all_gather x1, blocking collectives, local(): pieces = lax.all_gather(pieces, 'c', axis=0)  3.89 us
    ppermute x1, starting transfers between devices, local(): lax.ppermute(near[:width * blocks * 3 // 2], ('y', 'x', 'c'), neighbour_p...  2.22 us
  transfers between devices with their start and end apart: 4, of which 2 were waited for; matrix products, arithmetic and copies ran while one was open for 1% of the time, Pallas kernels for 5%

profile of v2, /device:TPU:1, one launch (start us, length us, event | category | flops | bytes accessed | tf_op | source)
XLA Modules:
  0.0 77.1 jit_solution(1034631013033933353)
XLA Ops:
  0.0 1.3 %shard_map.127 = (bf16[1024,256]{1,0:T(8,128)(2,1)S(1)}, bf16[128,128]{1,0:T(8,128)(2,1)S(1)}, f32[1,512]{1,0:T(1,128)S(1)}, bf16[3,512,128]{2,1,0:T(8,128)(2,1)S(1)}, bf16[2,128,128]{2,1,0:T(8,128)(2,1)S(1)}) custom-call(s32[1]{0:T(128)} %bitcast.half, s32[1]{0:T(128)} %bitcast.1.parity, bf16[512,512]{1,0:T(8,128)(2,1)} %refs_0_.2, ...), custom_call_target="tpu_custom_call" | custom-call | bytes 1048576 | tf_op jit(solution)/shard_map/pallas_call | solution.py:181
  1.3 16.1 %all_gather.15.whole = bf16[128,512]{1,0:T(8,128)(2,1)S(1)} all-gather(bf16[128,128]{1,0:T(8,128)(2,1)S(1)} %get-tuple-element.28), channel_id=1, replica_groups=mesh['z'=4,'y'=8,'x'=4,'h'=2,'c'=2] {'h','c'}, dimensions={1}, use_global_device_ids=true | all-gather | bytes 163840 | tf_op jit(solution)/shard_map/all_gather | solution.py:346
  17.4 0.4 shard_map.128
  17.8 0.8 %copy.17 = bf16[128,5,128]{2,1,0:T(8,128)(2,1)} copy(bf16[128,5,128]{2,0,1:T(8,128)(2,1)S(1)} %bitcast.17) | data formatting | bytes 327680 | tf_op jit(solution)/shard_map/optimization_barrier | solution.py:356
  18.6 14.5 %all-to-all-start = ((bf16[128,5,128]{2,1,0:T(8,128)(2,1)}), bf16[128,5,128]{2,1,0:T(8,128)(2,1)S(1)}, u32[]{:S(2)}, u32[]{:S(2)}) async-start(bf16[128,5,128]{2,1,0:T(8,128)(2,1)} %copy.17), calls=%async_computation | async-start | bytes 524288 | tf_op jit(solution)/shard_map/all_to_all | solution.py:359
  33.1 5.2 %collective-permute-start = (bf16[1024,256]{1,0:T(8,128)(2,1)S(1)}, bf16[1024,256]{1,0:T(8,128)(2,1)S(1)}, u32[]{:S(2)}, u32[]{:S(2)}) collective-permute-start(bf16[1024,256]{1,0:T(8,128)(2,1)S(1)} %get-tuple-element.45), channel_id=1, source_target_pairs={{0,258},{128,386},{256,2},{384,130},{2,256},{130,384},{258,0},{386... | collective-permute-start | bytes 1572872 | tf_op jit(solution)/shard_map/ppermute | solution.py:375
  38.3 1.5 %shard_map.129 = (bf16[512,256]{1,0:T(8,128)(2,1)S(1)}, bf16[512,512]{1,0:T(8,128)(2,1)S(1)}, bf16[128,512]{1,0:T(8,128)(2,1)S(1)}, f32[3,3,128]{2,1,0:T(4,128)S...) custom-call(s32[1]{0:T(128)} %bitcast.half, ...), custom_call_target="tpu_custom_call" | custom-call | bytes 1048576 | tf_op jit(solution)/shard_map/pallas_call | solution.py:181
  39.8 0.0 all-to-all-done
  39.9 2.0 %shard_map.130 = bf16[128,128]{1,0:T(8,128)(2,1)S(1)} custom-call(s32[1]{0:T(128)} %bitcast.5.mine, f32[3,3,128]{2,1,0:T(4,128)S(1)} %get-tuple-element.38.short_w, f32[2,128]{1,0:T(2,128)S(1)} %get-tuple-element.39.bias, bf16[5,128,128]{2,1,0:T(8,128)(2,1)S(1)} %bitcast.18, bf16[128,128]{1,0:T(8,128)(2,1)S(1)} %get-tuple-element.41.previous, ...), custom_call_target="tpu_custom_call" | custom-call | flops 536870912 | bytes 1048576 | tf_op jit(solution)/shard_map/pallas_call | solution.py:181
  41.9 0.7 copy.19
  42.6 20.4 %all-to-all-start.1 = ((bf16[256,1,128]{2,1,0:T(2,128)(2,1)}), bf16[256,1,128]{2,1,0:T(2,128)(2,1)S(1)}, u32[]{:S(2)}, u32[]{:S(2)}) async-start(bf16[256,1,128]{2,1,0:T(2,128)(2,1)} %copy.19), calls=%async_computation.1 | async-start | bytes 262144 | tf_op jit(solution)/shard_map/all_to_all | solution.py:389
  63.1 0.0 collective-permute-done.near
  63.1 2.2 %collective-permute-start.1 = (bf16[768,256]{1,0:T(8,128)(2,1)S(1)}, bf16[768,256]{1,0:T(8,128)(2,1)S(1)}, u32[]{:S(2)}, u32[]{:S(2)}) collective-permute-start(bf16[768,256]{1,0:T(8,128)(2,1)S(1)} %slice.4), channel_id=1, source_target_pairs={{0,4},{1,17},{4,0},{5,21},{8,12},{9,25},{12,8},{13,29},{16,20},{17... | collective-permute-start | bytes 1179656 | tf_op jit(solution)/shard_map/ppermute | solution.py:376
  65.4 1.4 %all-to-all-done.1 = bf16[256,1,128]{2,1,0:T(2,128)(2,1)S(1)} async-done(((bf16[256,1,128]{2,1,0:T(2,128)(2,1)}), bf16[256,1,128]{2,1,0:T(2,128)(2,1)S(1)}, u32[]{:S(2)}, u32[]{:S(2)}) %all-to-all-start.1) | async-done | bytes 65568 | tf_op jit(solution)/shard_map/all_to_all | solution.py:389
  66.8 0.2 shard_map.131
  67.0 4.4 %all-gather = f32[256,512]{1,0:T(8,128)S(1)} all-gather(f32[128,512]{1,0:T(8,128)S(1)} %shard_map.131), channel_id=2, replica_groups=mesh['z'=4,'y'=8,'x'=4,'h'=2,'c'=2] {'c'}, dimensions={0}, use_global_device_ids=true | all-gather | bytes 786432 | tf_op jit(solution)/shard_map/all_gather | solution.py:407
  71.4 0.5 collective-permute-done.1.far
  71.9 0.7 shard_map.132
  72.6 3.9 %all-gather.1 = bf16[4,128,128]{2,1,0:T(8,128)(2,1)S(1)} all-gather(bf16[2,128,128]{2,1,0:T(8,128)(2,1)S(1)} %get-tuple-element.50), channel_id=3, replica_groups=mesh['z'=4,'y'=8,'x'=4,'h'=2,'c'=2] {'c'}, dimensions={0}, use_global_device_ids=true | all-gather | bytes 196608 | tf_op jit(solution)/shard_map/all_gather | solution.py:423
  76.5 0.6 add_convert_fusion
  (5 shorter events, 0.1 us)
Async XLA Ops:
  18.6 21.2 %all-to-all-start = ((bf16[128,5,128]{2,1,0:T(8,128)(2,1)}), bf16[128,5,128]{2,1,0:T(8,128)(2,1)S(1)}, u32[]{:S(2)}, u32[]{:S(2)}) async-start(bf16[128,5,128]{2,1,0:T(8,128)(2,1)} %copy.17), calls=%async_computation | async-start | bytes 524288 | tf_op jit(solution)/shard_map/all_to_all | solution.py:359
  33.1 30.0 %collective-permute-start = (bf16[1024,256]{1,0:T(8,128)(2,1)S(1)}, bf16[1024,256]{1,0:T(8,128)(2,1)S(1)}, u32[]{:S(2)}, u32[]{:S(2)}) collective-permute-start(bf16[1024,256]{1,0:T(8,128)(2,1)S(1)} %get-tuple-element.45), channel_id=1, source_target_pairs={{0,258},{128,386},{256,2},{384,130},{2,256},{130,384},{258,0},{386... | collective-permute-start | bytes 1572872 | tf_op jit(solution)/shard_map/ppermute | solution.py:375
  42.6 24.1 %all-to-all-start.1 = ((bf16[256,1,128]{2,1,0:T(2,128)(2,1)}), bf16[256,1,128]{2,1,0:T(2,128)(2,1)S(1)}, u32[]{:S(2)}, u32[]{:S(2)}) async-start(bf16[256,1,128]{2,1,0:T(2,128)(2,1)} %copy.19), calls=%async_computation.1 | async-start | bytes 262144 | tf_op jit(solution)/shard_map/all_to_all | solution.py:389
  63.1 8.8 %collective-permute-start.1 = (bf16[768,256]{1,0:T(8,128)(2,1)S(1)}, bf16[768,256]{1,0:T(8,128)(2,1)S(1)}, u32[]{:S(2)}, u32[]{:S(2)}) collective-permute-start(bf16[768,256]{1,0:T(8,128)(2,1)S(1)} %slice.4), channel_id=1, source_target_pairs={{0,4},{1,17},{4,0},{5,21},{8,12},{9,25},{12,8},{13,29},{16,20},{17... | collective-permute-start | bytes 1179656 | tf_op jit(solution)/shard_map/ppermute | solution.py:376

commit v3 on v2

--- a/solution.py
+++ b/solution.py
@@ -36,13 +36,8 @@
 
 
 def second_ranks(deep, high, wide):
-    return [
-        (((1 - h) * deep + z) * high + (y + high // 2) % high) * wide + (x + wide // 2) % wide
-        for h in range(2)
-        for z in range(deep)
-        for y in range(high)
-        for x in range(wide)
-    ]
+    ranks = first_ranks(deep, high, wide)
+    return [len(ranks) + rank for rank in ranks] + ranks
 
 
 def previous_rows(times):
@@ -90,11 +85,6 @@
 def delayed(values, above, by):
     col = lax.broadcasted_iota(jnp.int32, values.shape, 1)
     return jnp.where(col >= by, pltpu.roll(values, by, 1), pltpu.roll(above, by, 1))
-
-
-def turned_blocks(values):
-    step = values.shape[0] // DEEP
-    return [values[k * step : (k + 1) * step] for k in reversed(range(DEEP))]
 
 
 def round_bf16(values):
@@ -168,8 +158,7 @@
     gated = (short(1).astype(jnp.float32) * round_bf16(first)).astype(jnp.bfloat16)
     (signal,) = forward([gated])
     second = inverse(signal, response_two) + scalars[10] * gated.astype(jnp.float32)
-    product = (short(2).astype(jnp.float32) * round_bf16(second)).astype(jnp.bfloat16)
-    mixed[...] = jnp.concatenate(turned_blocks(product), axis=0)
+    mixed[...] = (short(2).astype(jnp.float32) * round_bf16(second)).astype(jnp.bfloat16)
 
 
 def call(
@@ -262,7 +251,7 @@
     weights = (jnp.where(low, own[...], other), jnp.where(low, other, own[...]))
     parts = [
         lax.dot_general(
-            jnp.concatenate(turned_blocks(arrived[1 - k]), axis=0),
+            arrived[1 - k],
             weights[k],
             (((0,), (0,)), ((), ())),
             preferred_element_type=jnp.float32,
@@ -272,9 +261,9 @@
     partial[...] = parts[0] + parts[1]
 
 
-def mlp_kernel(place, parity, whole, shares, gain, w_up, w_down, near, far, pieces, own):
-    count, _, width = pieces.shape
+def mlp_kernel(place, whole, shares, gain, w_up, w_down, near, own, normed, partial):
     units = whole.shape[1]
+    width = own.shape[1]
     half_units = units // 2
     share = shares[0] + shares[1]
     middle = (whole[...].astype(jnp.float32) + share).astype(jnp.bfloat16)
@@ -282,15 +271,21 @@
     for k in range(1, units // width):
         mine = jnp.where(place[0] == k, middle[:, k * width : (k + 1) * width], mine)
     own[...] = mine
-    normed = rms_norm(middle, gain[...])
-    hidden = jax.nn.gelu(dot(normed, w_up[...])).astype(jnp.bfloat16)
-    partial = dot(hidden, w_down[...])
-    for part in (near, far):
-        hidden = jax.nn.gelu(dot(normed, part[:units])).astype(jnp.bfloat16)
-        partial = partial + dot(hidden, part[units : units + half_units])
-    partial = partial.astype(jnp.bfloat16)
+    scaled = rms_norm(middle, gain[...])
+    normed[...] = scaled
+    hidden = jax.nn.gelu(dot(scaled, w_up[...])).astype(jnp.bfloat16)
+    total = dot(hidden, w_down[...])
+    hidden = jax.nn.gelu(dot(scaled, near[:units])).astype(jnp.bfloat16)
+    partial[...] = total + dot(hidden, near[units : units + half_units])
+
+
+def far_kernel(normed, partial, far, pieces):
+    count, _, width = pieces.shape
+    units = normed.shape[1]
+    hidden = jax.nn.gelu(dot(normed[...], far[:units])).astype(jnp.bfloat16)
+    total = (partial[...] + dot(hidden, far[units:])).astype(jnp.bfloat16)
     for k in range(count):
-        pieces[k] = partial[:, k * width : (k + 1) * width]
+        pieces[k] = total[:, k * width : (k + 1) * width]
 
 
 def other_half_pairs():
@@ -405,20 +400,25 @@
         scalars=1,
     )
     shares = lax.all_gather(partial, "c", axis=0)
-    pieces, own = call(
+    own, normed, partial = call(
         mlp_kernel,
-        (shape((2, samples, width), jnp.bfloat16), shape((samples, width), jnp.bfloat16)),
+        (
+            shape((samples, width), jnp.bfloat16),
+            shape((samples, blocks * width), jnp.bfloat16),
+            shape((samples, part), jnp.float32),
+        ),
         2**28,
         place,
-        parity,
         whole,
         shares,
         gain_mlp,
         w_up,
         w_down,
         near,
-        far,
-        scalars=2,
+        scalars=1,
+    )
+    pieces = call(
+        far_kernel, shape((2, samples, width), jnp.bfloat16), 2**27, normed, partial, far
     )
     pieces = lax.all_gather(pieces, "c", axis=0)
     pieces = lax.dynamic_index_in_dim(pieces, place[0] % 2, 1, keepdims=False)

time: 77.5 us -> 76.5 us (0.987)
  starting transfers between devices: 42.4 us -> 41 us
    all_to_all x1, starting transfers between devices: 20.4 us -> 19.1 us  [local(): lax.all_to_all(doubled, ('h',) + SEQ, split_axis=0, concat_axis=0, tiled=...]
    all_gather x1, blocking collectives: 4.38 us -> 5.27 us  [local(): shares = lax.all_gather(partial, 'c', axis=0)]
    pallas_call x6 -> x7, Pallas kernels: 6.08 us -> 6.38 us  [call(): pl.pallas_call(kernel, out_shape=out_shape, in_specs=[smem] * scalars + [...]
  transfers between devices with their start and end apart: 4 -> 4, of which waited for: 2 -> 1; matrix products, arithmetic and copies ran while one was open for 1% -> 1% of each run, Pallas kernels for 5% -> 6%
where the time goes in v3:
time: 76.5 us; the launch traced here: 76.2 us
  starting transfers between devices  41 us (54%)
  blocking collectives  24.7 us (32%)
  Pallas kernels  6.38 us (8%)
  waiting for transfers between devices  1.72 us (2%)
  local copies, waits for them, and re-layouts  1.64 us (2%)
    all_to_all x1, starting transfers between devices, local(): lax.all_to_all(doubled, ('h',) + SEQ, split_axis=0, concat_axis=0, tiled=...  19.1 us
    all_gather x1, blocking collectives, local(): whole = lax.all_gather(tokens, CH, axis=1, tiled=True)  16.1 us
    all_to_all x1, starting transfers between devices, local(): lax.all_to_all(outgoing, SEQ, split_axis=0, concat_axis=0, tiled=True, ax...  14.5 us
    pallas_call x7, Pallas kernels, call(): pl.pallas_call(kernel, out_shape=out_shape, in_specs=[smem] * scalars + [...  6.38 us
    all_gather x1, blocking collectives, local(): shares = lax.all_gather(partial, 'c', axis=0)  5.27 us
    ppermute x1, starting transfers between devices, local(): near = lax.ppermute(sent, ('z', 'h'), other_half_pairs())  5.17 us
    all_gather x1, blocking collectives, local(): pieces = lax.all_gather(pieces, 'c', axis=0)  3.38 us
    ppermute x1, starting transfers between devices, local(): lax.ppermute(near[:width * blocks * 3 // 2], ('y', 'x', 'c'), neighbour_p...  2.2 us
  transfers between devices with their start and end apart: 4, of which 1 were waited for; matrix products, arithmetic and copies ran while one was open for 1% of the time, Pallas kernels for 6%

profile of v3, /device:TPU:1, one launch (start us, length us, event | category | flops | bytes accessed | tf_op | source)
XLA Modules:
  0.0 76.2 jit_solution(5604854523771249927)
XLA Ops:
  0.0 1.3 %shard_map.127 = (bf16[1024,256]{1,0:T(8,128)(2,1)S(1)}, bf16[128,128]{1,0:T(8,128)(2,1)S(1)}, f32[1,512]{1,0:T(1,128)S(1)}, bf16[3,512,128]{2,1,0:T(8,128)(2,1)S(1)}, bf16[2,128,128]{2,1,0:T(8,128)(2,1)S(1)}) custom-call(s32[1]{0:T(128)} %bitcast.half, s32[1]{0:T(128)} %bitcast.1.parity, bf16[512,512]{1,0:T(8,128)(2,1)} %refs_0_.2, ...), custom_call_target="tpu_custom_call" | custom-call | bytes 1048576 | tf_op jit(solution)/shard_map/pallas_call | solution.py:170
  1.3 16.1 %all_gather.15.whole = bf16[128,512]{1,0:T(8,128)(2,1)S(1)} all-gather(bf16[128,128]{1,0:T(8,128)(2,1)S(1)} %get-tuple-element.28), channel_id=1, replica_groups=mesh['z'=4,'y'=8,'x'=4,'h'=2,'c'=2] {'h','c'}, dimensions={1}, use_global_device_ids=true | all-gather | bytes 163840 | tf_op jit(solution)/shard_map/all_gather | solution.py:341
  17.4 0.4 shard_map.128
  17.8 0.8 %copy.17 = bf16[128,5,128]{2,1,0:T(8,128)(2,1)} copy(bf16[128,5,128]{2,0,1:T(8,128)(2,1)S(1)} %bitcast.17) | data formatting | bytes 327680 | tf_op jit(solution)/shard_map/optimization_barrier | solution.py:351
  18.6 14.5 %all-to-all-start = ((bf16[128,5,128]{2,1,0:T(8,128)(2,1)}), bf16[128,5,128]{2,1,0:T(8,128)(2,1)S(1)}, u32[]{:S(2)}, u32[]{:S(2)}) async-start(bf16[128,5,128]{2,1,0:T(8,128)(2,1)} %copy.17), calls=%async_computation | async-start | bytes 524288 | tf_op jit(solution)/shard_map/all_to_all | solution.py:354
  33.1 5.2 %collective-permute-start = (bf16[1024,256]{1,0:T(8,128)(2,1)S(1)}, bf16[1024,256]{1,0:T(8,128)(2,1)S(1)}, u32[]{:S(2)}, u32[]{:S(2)}) collective-permute-start(bf16[1024,256]{1,0:T(8,128)(2,1)S(1)} %get-tuple-element.44), channel_id=1, source_target_pairs={{0,258},{128,386},{256,2},{384,130},{2,256},{130,384},{258,0},{386... | collective-permute-start | bytes 1572872 | tf_op jit(solution)/shard_map/ppermute | solution.py:370
  38.3 1.5 %shard_map.129 = (bf16[512,256]{1,0:T(8,128)(2,1)S(1)}, bf16[512,512]{1,0:T(8,128)(2,1)S(1)}, bf16[128,512]{1,0:T(8,128)(2,1)S(1)}, f32[3,3,128]{2,1,0:T(4,128)S...) custom-call(s32[1]{0:T(128)} %bitcast.half, ...), custom_call_target="tpu_custom_call" | custom-call | bytes 1048576 | tf_op jit(solution)/shard_map/pallas_call | solution.py:170
  39.8 0.0 all-to-all-done
  39.9 2.0 %shard_map.130 = bf16[128,128]{1,0:T(8,128)(2,1)S(1)} custom-call(s32[1]{0:T(128)} %bitcast.5.mine, f32[3,3,128]{2,1,0:T(4,128)S(1)} %get-tuple-element.37.short_w, f32[2,128]{1,0:T(2,128)S(1)} %get-tuple-element.38.bias, bf16[5,128,128]{2,1,0:T(8,128)(2,1)S(1)} %bitcast.18, bf16[128,128]{1,0:T(8,128)(2,1)S(1)} %get-tuple-element.40.previous, ...), custom_call_target="tpu_custom_call" | custom-call | flops 536870912 | bytes 1048576 | tf_op jit(solution)/shard_map/pallas_call | solution.py:170
  41.9 0.7 copy.19
  42.6 19.1 %all-to-all-start.1 = ((bf16[256,1,128]{2,1,0:T(2,128)(2,1)}), bf16[256,1,128]{2,1,0:T(2,128)(2,1)S(1)}, u32[]{:S(2)}, u32[]{:S(2)}) async-start(bf16[256,1,128]{2,1,0:T(2,128)(2,1)} %copy.19), calls=%async_computation.1 | async-start | bytes 262144 | tf_op jit(solution)/shard_map/all_to_all | solution.py:384
  61.7 0.0 collective-permute-done.near
  61.7 2.2 %collective-permute-start.1 = (bf16[768,256]{1,0:T(8,128)(2,1)S(1)}, bf16[768,256]{1,0:T(8,128)(2,1)S(1)}, u32[]{:S(2)}, u32[]{:S(2)}) collective-permute-start(bf16[768,256]{1,0:T(8,128)(2,1)S(1)} %slice.4), channel_id=1, source_target_pairs={{0,4},{1,17},{4,0},{5,21},{8,12},{9,25},{12,8},{13,29},{16,20},{17... | collective-permute-start | bytes 1179656 | tf_op jit(solution)/shard_map/ppermute | solution.py:371
  64.0 1.7 %all-to-all-done.1 = bf16[256,1,128]{2,1,0:T(2,128)(2,1)S(1)} async-done(((bf16[256,1,128]{2,1,0:T(2,128)(2,1)}), bf16[256,1,128]{2,1,0:T(2,128)(2,1)S(1)}, u32[]{:S(2)}, u32[]{:S(2)}) %all-to-all-start.1) | async-done | bytes 65568 | tf_op jit(solution)/shard_map/all_to_all | solution.py:384
  65.7 0.3 shard_map.131
  65.9 5.3 %all-gather = f32[256,512]{1,0:T(8,128)S(1)} all-gather(f32[128,512]{1,0:T(8,128)S(1)} %shard_map.131), channel_id=2, replica_groups=mesh['z'=4,'y'=8,'x'=4,'h'=2,'c'=2] {'c'}, dimensions={0}, use_global_device_ids=true | all-gather | bytes 786432 | tf_op jit(solution)/shard_map/all_gather | solution.py:402
  71.2 0.6 shard_map.132
  71.8 0.0 collective-permute-done.1.far
  71.8 0.4 shard_map.133
  72.2 3.4 %all-gather.1 = bf16[4,128,128]{2,1,0:T(8,128)(2,1)S(1)} all-gather(bf16[2,128,128]{2,1,0:T(8,128)(2,1)S(1)} %shard_map.133), channel_id=3, replica_groups=mesh['z'=4,'y'=8,'x'=4,'h'=2,'c'=2] {'c'}, dimensions={0}, use_global_device_ids=true | all-gather | bytes 196608 | tf_op jit(solution)/shard_map/all_gather | solution.py:423
  75.6 0.6 add_convert_fusion
  (5 shorter events, 0.1 us)
Async XLA Ops:
  18.6 21.2 %all-to-all-start = ((bf16[128,5,128]{2,1,0:T(8,128)(2,1)}), bf16[128,5,128]{2,1,0:T(8,128)(2,1)S(1)}, u32[]{:S(2)}, u32[]{:S(2)}) async-start(bf16[128,5,128]{2,1,0:T(8,128)(2,1)} %copy.17), calls=%async_computation | async-start | bytes 524288 | tf_op jit(solution)/shard_map/all_to_all | solution.py:354
  33.1 28.6 %collective-permute-start = (bf16[1024,256]{1,0:T(8,128)(2,1)S(1)}, bf16[1024,256]{1,0:T(8,128)(2,1)S(1)}, u32[]{:S(2)}, u32[]{:S(2)}) collective-permute-start(bf16[1024,256]{1,0:T(8,128)(2,1)S(1)} %get-tuple-element.44), channel_id=1, source_target_pairs={{0,258},{128,386},{256,2},{384,130},{2,256},{130,384},{258,0},{386... | collective-permute-start | bytes 1572872 | tf_op jit(solution)/shard_map/ppermute | solution.py:370
  42.6 23.0 %all-to-all-start.1 = ((bf16[256,1,128]{2,1,0:T(2,128)(2,1)}), bf16[256,1,128]{2,1,0:T(2,128)(2,1)S(1)}, u32[]{:S(2)}, u32[]{:S(2)}) async-start(bf16[256,1,128]{2,1,0:T(2,128)(2,1)} %copy.19), calls=%async_computation.1 | async-start | bytes 262144 | tf_op jit(solution)/shard_map/all_to_all | solution.py:384
  61.7 10.1 %collective-permute-start.1 = (bf16[768,256]{1,0:T(8,128)(2,1)S(1)}, bf16[768,256]{1,0:T(8,128)(2,1)S(1)}, u32[]{:S(2)}, u32[]{:S(2)}) collective-permute-start(bf16[768,256]{1,0:T(8,128)(2,1)S(1)} %slice.4), channel_id=1, source_target_pairs={{0,4},{1,17},{4,0},{5,21},{8,12},{9,25},{12,8},{13,29},{16,20},{17... | collective-permute-start | bytes 1179656 | tf_op jit(solution)/shard_map/ppermute | solution.py:371

commit v4 on v3

--- a/solution.py
+++ b/solution.py
@@ -28,7 +28,7 @@
 
 def first_ranks(deep, high, wide):
     return [
-        ((deep - 1 - z) * high + (y + high // 2) % high) * wide + (x + wide // 2) % wide
+        ((deep - 1 - z) * high + (y + high // 2) % high) * wide + (x + wide - 1) % wide
         for z in range(deep)
         for y in range(high)
         for x in range(wide)
@@ -92,8 +92,9 @@
 
 
 def channel_kernel(mine, short_w, bias, u, previous, products, turn, mixed):
-    rows, cols = u.shape[1], u.shape[2]
-    above = dot(previous[...], jnp.concatenate([u[0], u[1], u[2]], axis=1))
+    rows, cols = u.shape[1], u.shape[2] // 3
+    projected = u[0]
+    above = dot(previous[...], projected)
     outer, inner_high, inner_low = products[0], products[1], products[2]
     back_high, back_low = products[3, :rows], products[3, rows:]
     turn_real, turn_imag = turn[0], turn[1]
@@ -103,7 +104,7 @@
     scalars = [scalars[k : k + 1] for k in range(scalars.shape[0])]
 
     def short(k):
-        values = u[k].astype(jnp.float32)
+        values = projected[:, k * cols : (k + 1) * cols].astype(jnp.float32)
         total = scalars[3 * k] * values
         past = above[:, k * cols : (k + 1) * cols]
         total = total + scalars[3 * k + 1] * delayed(values, past, 1)
@@ -153,7 +154,7 @@
         return side[:, :cols] + side[:, cols:] + dot(back_low, high)
 
     v = short(0)
-    signal, response_one, response_two = forward([v, u[3], u[4]])
+    signal, response_one, response_two = forward([v, u[1, :, :cols], u[1, :, cols : 2 * cols]])
     first = inverse(signal, response_one) + scalars[9] * v.astype(jnp.float32)
     gated = (short(1).astype(jnp.float32) * round_bf16(first)).astype(jnp.bfloat16)
     (signal,) = forward([gated])
@@ -234,13 +235,12 @@
 
 def project_kernel(whole, gain, w_in, filters, outgoing):
     normed = rms_norm(whole[...], gain[...])
-    count = w_in.shape[0]
+    count, _, width = w_in.shape
     for k in range(count):
-        outgoing[k] = lax.dot_general(
+        outgoing[0, :, k * width : (k + 1) * width] = lax.dot_general(
             w_in[k], normed, (((0,), (1,)), ((), ())), preferred_element_type=jnp.float32
         ).astype(jnp.bfloat16)
-    for k in range(filters.shape[0]):
-        outgoing[count + k] = filters[k]
+    outgoing[1] = jnp.concatenate([filters[0], filters[1], jnp.zeros_like(filters[0])], axis=1)
 
 
 def out_kernel(half, arrived, own, near, partial):
@@ -303,8 +303,8 @@
     pairs = []
     for y in range(high):
         for x in range(wide):
-            pairs.append(((y * wide + x) * 2, (y * wide + (x ^ 1)) * 2))
-            pairs.append(((y * wide + x) * 2 + 1, ((y ^ 1) * wide + x) * 2 + 1))
+            pairs.append(((y * wide + x) * 2, ((y ^ 1) * wide + x) * 2))
+            pairs.append(((y * wide + x) * 2 + 1, (y * wide + (x ^ 1)) * 2 + 1))
     return pairs
 
 
@@ -315,11 +315,11 @@
     shape = jax.ShapeDtypeStruct
     place_z, place_y, place_x = (lax.axis_index(axis) for axis in SEQ)
     mine = (DEEP - 1 - place_z) * HIGH + (place_y + HIGH // 2) % HIGH
-    mine = (mine * WIDE + (place_x + WIDE // 2) % WIDE).astype(jnp.int32)[None]
+    mine = (mine * WIDE + (place_x + 1) % WIDE).astype(jnp.int32)[None]
     ranks = first_ranks(DEEP, HIGH, WIDE)
     place = lax.axis_index(CH).astype(jnp.int32)[None]
     half = lax.axis_index("h").astype(jnp.int32)[None]
-    side = jnp.where(lax.axis_index("c") == 0, lax.axis_index("x"), lax.axis_index("y"))
+    side = jnp.where(lax.axis_index("c") == 0, lax.axis_index("y"), lax.axis_index("x"))
     parity = (side % 2).astype(jnp.int32)[None]
     tables = [previous_rows(ranks), *transform_tables(shards, samples, ranks)]
     tables = [jnp.asarray(table) for table in tables]
@@ -341,7 +341,7 @@
     whole = lax.all_gather(tokens, CH, axis=1, tiled=True)
     outgoing = call(
         project_kernel,
-        shape((5, width, samples), jnp.bfloat16),
+        shape((2, width, 3 * samples), jnp.bfloat16),
         2**26,
         whole,
         gain_mix,

time: 76.5 us -> 76.3 us (level)
  starting transfers between devices: 41 us -> 39.9 us
    ppermute x1, waiting for transfers between devices: 0.03 us -> 2.35 us  [local(): near = lax.ppermute(sent, ('z', 'h'), other_half_pairs())]
    all_to_all x1, waiting for transfers between devices: 1.68 us -> 0.01 us  [local(): lax.all_to_all(doubled, ('h',) + SEQ, split_axis=0, concat_axis=0, tiled=...]
    all_gather x1, blocking collectives: 5.27 us -> 6.49 us  [local(): shares = lax.all_gather(partial, 'c', axis=0)]
    all_to_all x1, starting transfers between devices: 19.1 us -> 17.9 us  [local(): lax.all_to_all(doubled, ('h',) + SEQ, split_axis=0, concat_axis=0, tiled=...]
    all_gather x1, blocking collectives: 3.38 us -> 2.36 us  [local(): pieces = lax.all_gather(pieces, 'c', axis=0)]
where the time goes in v4:
time: 76.3 us; the launch traced here: 76 us
  starting transfers between devices  39.9 us (52%)
  blocking collectives  24.9 us (33%)
  Pallas kernels  6.39 us (8%)
  waiting for transfers between devices  2.36 us (3%)
  local copies, waits for them, and re-layouts  1.68 us (2%)
    all_to_all x1, starting transfers between devices, local(): lax.all_to_all(doubled, ('h',) + SEQ, split_axis=0, concat_axis=0, tiled=...  17.9 us
    all_gather x1, blocking collectives, local(): whole = lax.all_gather(tokens, CH, axis=1, tiled=True)  16.1 us
    all_to_all x1, starting transfers between devices, local(): lax.all_to_all(outgoing, SEQ, split_axis=0, concat_axis=0, tiled=True, ax...  14.3 us
    all_gather x1, blocking collectives, local(): shares = lax.all_gather(partial, 'c', axis=0)  6.49 us
    pallas_call x7, Pallas kernels, call(): pl.pallas_call(kernel, out_shape=out_shape, in_specs=[smem] * scalars + [...  6.39 us
    ppermute x1, starting transfers between devices, local(): near = lax.ppermute(sent, ('z', 'h'), other_half_pairs())  5.18 us
    ppermute x1, starting transfers between devices, local(): lax.ppermute(near[:width * blocks * 3 // 2], ('y', 'x', 'c'), neighbour_p...  2.5 us
    all_gather x1, blocking collectives, local(): pieces = lax.all_gather(pieces, 'c', axis=0)  2.36 us
  transfers between devices with their start and end apart: 4, of which 1 were waited for; matrix products, arithmetic and copies ran while one was open for 1% of the time, Pallas kernels for 6%

profile of v4, /device:TPU:1, one launch (start us, length us, event | category | flops | bytes accessed | tf_op | source)
XLA Modules:
  0.0 76.0 jit_solution(15553133399559972919)
XLA Ops:
  0.0 1.3 %shard_map.127 = (bf16[1024,256]{1,0:T(8,128)(2,1)S(1)}, bf16[128,128]{1,0:T(8,128)(2,1)S(1)}, f32[1,512]{1,0:T(1,128)S(1)}, bf16[3,512,128]{2,1,0:T(8,128)(2,1)S(1)}, bf16[2,128,128]{2,1,0:T(8,128)(2,1)S(1)}) custom-call(s32[1]{0:T(128)} %bitcast.half, s32[1]{0:T(128)} %bitcast.1.parity, bf16[512,512]{1,0:T(8,128)(2,1)} %refs_0_.2, ...), custom_call_target="tpu_custom_call" | custom-call | bytes 1048576 | tf_op jit(solution)/shard_map/pallas_call | solution.py:171
  1.3 16.1 %all_gather.15.whole = bf16[128,512]{1,0:T(8,128)(2,1)S(1)} all-gather(bf16[128,128]{1,0:T(8,128)(2,1)S(1)} %get-tuple-element.28), channel_id=1, replica_groups=mesh['z'=4,'y'=8,'x'=4,'h'=2,'c'=2] {'h','c'}, dimensions={1}, use_global_device_ids=true | all-gather | bytes 163840 | tf_op jit(solution)/shard_map/all_gather | solution.py:341
  17.4 0.4 shard_map.128
  17.8 0.9 %copy.17 = bf16[128,2,384]{2,1,0:T(2,128)(2,1)} copy(bf16[128,2,384]{2,0,1:T(8,128)(2,1)S(1)} %bitcast.17) | data formatting | bytes 393216 | tf_op jit(solution)/shard_map/optimization_barrier | solution.py:351
  18.6 14.3 %all-to-all-start = ((bf16[128,2,384]{2,1,0:T(2,128)(2,1)}), bf16[128,2,384]{2,1,0:T(2,128)(2,1)S(1)}, u32[]{:S(2)}, u32[]{:S(2)}) async-start(bf16[128,2,384]{2,1,0:T(2,128)(2,1)} %copy.17), calls=%async_computation | async-start | bytes 393216 | tf_op jit(solution)/shard_map/all_to_all | solution.py:354
  32.9 5.2 %collective-permute-start = (bf16[1024,256]{1,0:T(8,128)(2,1)S(1)}, bf16[1024,256]{1,0:T(8,128)(2,1)S(1)}, u32[]{:S(2)}, u32[]{:S(2)}) collective-permute-start(bf16[1024,256]{1,0:T(8,128)(2,1)S(1)} %get-tuple-element.44), channel_id=1, source_target_pairs={{0,258},{128,386},{256,2},{384,130},{2,256},{130,384},{258,0},{386... | collective-permute-start | bytes 1572872 | tf_op jit(solution)/shard_map/ppermute | solution.py:370
  38.1 1.5 %shard_map.129 = (bf16[512,256]{1,0:T(8,128)(2,1)S(1)}, bf16[512,512]{1,0:T(8,128)(2,1)S(1)}, bf16[128,512]{1,0:T(8,128)(2,1)S(1)}, f32[3,3,128]{2,1,0:T(4,128)S...) custom-call(s32[1]{0:T(128)} %bitcast.half, ...), custom_call_target="tpu_custom_call" | custom-call | bytes 1048576 | tf_op jit(solution)/shard_map/pallas_call | solution.py:171
  39.6 0.0 all-to-all-done
  39.6 2.0 %shard_map.130 = bf16[128,128]{1,0:T(8,128)(2,1)S(1)} custom-call(s32[1]{0:T(128)} %bitcast.5.mine, f32[3,3,128]{2,1,0:T(4,128)S(1)} %get-tuple-element.37.short_w, f32[2,128]{1,0:T(2,128)S(1)} %get-tuple-element.38.bias, bf16[2,128,384]{2,1,0:T(8,128)(2,1)S(1)} %bitcast.18, bf16[128,128]{1,0:T(8,128)(2,1)S(1)} %get-tuple-element.40.previous, ...), custom_call_target="tpu_custom_call" | custom-call | flops 536870912 | bytes 1048576 | tf_op jit(solution)/shard_map/pallas_call | solution.py:171
  41.6 0.7 copy.19
  42.4 17.9 %all-to-all-start.1 = ((bf16[256,1,128]{2,1,0:T(2,128)(2,1)}), bf16[256,1,128]{2,1,0:T(2,128)(2,1)S(1)}, u32[]{:S(2)}, u32[]{:S(2)}) async-start(bf16[256,1,128]{2,1,0:T(2,128)(2,1)} %copy.19), calls=%async_computation.1 | async-start | bytes 262144 | tf_op jit(solution)/shard_map/all_to_all | solution.py:384
  60.3 2.4 %collective-permute-done.near = bf16[1024,256]{1,0:T(8,128)(2,1)S(1)} collective-permute-done((bf16[1024,256]{1,0:T(8,128)(2,1)S(1)}, bf16[1024,256]{1,0:T(8,128)(2,1)S(1)}, u32[]{:S(2)}, u32[]{:S(2)}) %collective-permute-start) | collective-permute-done | bytes 524320 | tf_op jit(solution)/shard_map/ppermute | solution.py:370
  62.7 2.5 %collective-permute-start.1 = (bf16[768,256]{1,0:T(8,128)(2,1)S(1)}, bf16[768,256]{1,0:T(8,128)(2,1)S(1)}, u32[]{:S(2)}, u32[]{:S(2)}) collective-permute-start(bf16[768,256]{1,0:T(8,128)(2,1)S(1)} %slice.4), channel_id=1, source_target_pairs={{0,16},{1,5},{4,20},{5,1},{8,24},{9,13},{12,28},{13,9},{16,0},{17,... | collective-permute-start | bytes 1179656 | tf_op jit(solution)/shard_map/ppermute | solution.py:371
  65.2 0.0 all-to-all-done.1
  65.3 0.3 shard_map.131
  65.5 6.5 %all-gather = f32[256,512]{1,0:T(8,128)S(1)} all-gather(f32[128,512]{1,0:T(8,128)S(1)} %shard_map.131), channel_id=2, replica_groups=mesh['z'=4,'y'=8,'x'=4,'h'=2,'c'=2] {'c'}, dimensions={0}, use_global_device_ids=true | all-gather | bytes 786432 | tf_op jit(solution)/shard_map/all_gather | solution.py:402
  72.0 0.6 shard_map.132
  72.6 0.0 collective-permute-done.1.far
  72.6 0.4 shard_map.133
  73.0 2.4 %all-gather.1 = bf16[4,128,128]{2,1,0:T(8,128)(2,1)S(1)} all-gather(bf16[2,128,128]{2,1,0:T(8,128)(2,1)S(1)} %shard_map.133), channel_id=3, replica_groups=mesh['z'=4,'y'=8,'x'=4,'h'=2,'c'=2] {'c'}, dimensions={0}, use_global_device_ids=true | all-gather | bytes 196608 | tf_op jit(solution)/shard_map/all_gather | solution.py:423
  75.4 0.6 add_convert_fusion
  (5 shorter events, 0.1 us)
Async XLA Ops:
  18.6 21.0 %all-to-all-start = ((bf16[128,2,384]{2,1,0:T(2,128)(2,1)}), bf16[128,2,384]{2,1,0:T(2,128)(2,1)S(1)}, u32[]{:S(2)}, u32[]{:S(2)}) async-start(bf16[128,2,384]{2,1,0:T(2,128)(2,1)} %copy.17), calls=%async_computation | async-start | bytes 393216 | tf_op jit(solution)/shard_map/all_to_all | solution.py:354
  32.9 29.8 %collective-permute-start = (bf16[1024,256]{1,0:T(8,128)(2,1)S(1)}, bf16[1024,256]{1,0:T(8,128)(2,1)S(1)}, u32[]{:S(2)}, u32[]{:S(2)}) collective-permute-start(bf16[1024,256]{1,0:T(8,128)(2,1)S(1)} %get-tuple-element.44), channel_id=1, source_target_pairs={{0,258},{128,386},{256,2},{384,130},{2,256},{130,384},{258,0},{386... | collective-permute-start | bytes 1572872 | tf_op jit(solution)/shard_map/ppermute | solution.py:370
  42.4 22.8 %all-to-all-start.1 = ((bf16[256,1,128]{2,1,0:T(2,128)(2,1)}), bf16[256,1,128]{2,1,0:T(2,128)(2,1)S(1)}, u32[]{:S(2)}, u32[]{:S(2)}) async-start(bf16[256,1,128]{2,1,0:T(2,128)(2,1)} %copy.19), calls=%async_computation.1 | async-start | bytes 262144 | tf_op jit(solution)/shard_map/all_to_all | solution.py:384
  62.7 9.9 %collective-permute-start.1 = (bf16[768,256]{1,0:T(8,128)(2,1)S(1)}, bf16[768,256]{1,0:T(8,128)(2,1)S(1)}, u32[]{:S(2)}, u32[]{:S(2)}) collective-permute-start(bf16[768,256]{1,0:T(8,128)(2,1)S(1)} %slice.4), channel_id=1, source_target_pairs={{0,16},{1,5},{4,20},{5,1},{8,24},{9,13},{12,28},{13,9},{16,0},{17,... | collective-permute-start | bytes 1179656 | tf_op jit(solution)/shard_map/ppermute | solution.py:371

commit v5 on v4

--- a/solution.py
+++ b/solution.py
@@ -154,7 +154,9 @@
         return side[:, :cols] + side[:, cols:] + dot(back_low, high)
 
     v = short(0)
-    signal, response_one, response_two = forward([v, u[1, :, :cols], u[1, :, cols : 2 * cols]])
+    (response_one,) = forward([u[1, :, :cols]])
+    (response_two,) = forward([u[1, :, cols : 2 * cols]])
+    (signal,) = forward([v])
     first = inverse(signal, response_one) + scalars[9] * v.astype(jnp.float32)
     gated = (short(1).astype(jnp.float32) * round_bf16(first)).astype(jnp.bfloat16)
     (signal,) = forward([gated])

time: 76.3 us -> 76.6 us (level)
  transfers between devices with their start and end apart: 4 -> 4, of which waited for: 1 -> 1; matrix products, arithmetic and copies ran while one was open for 1% -> 1% of each run, Pallas kernels for 6% -> 5%
where the time goes in v5:
time: 76.6 us; the launch traced here: 76.3 us
  starting transfers between devices  39.9 us (52%)
  blocking collectives  24.9 us (33%)
  Pallas kernels  6.2 us (8%)
  waiting for transfers between devices  2.87 us (4%)
  local copies, waits for them, and re-layouts  1.68 us (2%)
    all_to_all x1, starting transfers between devices, local(): lax.all_to_all(doubled, ('h',) + SEQ, split_axis=0, concat_axis=0, tiled=...  17.9 us
    all_gather x1, blocking collectives, local(): whole = lax.all_gather(tokens, CH, axis=1, tiled=True)  16.1 us
    all_to_all x1, starting transfers between devices, local(): lax.all_to_all(outgoing, SEQ, split_axis=0, concat_axis=0, tiled=True, ax...  14.3 us
    pallas_call x7, Pallas kernels, call(): pl.pallas_call(kernel, out_shape=out_shape, in_specs=[smem] * scalars + [...  6.2 us
    all_gather x1, blocking collectives, local(): shares = lax.all_gather(partial, 'c', axis=0)  5.96 us
    ppermute x1, starting transfers between devices, local(): near = lax.ppermute(sent, ('z', 'h'), other_half_pairs())  5.18 us
    ppermute x1, waiting for transfers between devices, local(): near = lax.ppermute(sent, ('z', 'h'), other_half_pairs())  2.86 us
    all_gather x1, blocking collectives, local(): pieces = lax.all_gather(pieces, 'c', axis=0)  2.82 us
  transfers between devices with their start and end apart: 4, of which 1 were waited for; matrix products, arithmetic and copies ran while one was open for 1% of the time, Pallas kernels for 5%

profile of v5, /device:TPU:1, one launch (start us, length us, event | category | flops | bytes accessed | tf_op | source)
XLA Modules:
  0.0 76.3 jit_solution(3276439183343126965)
XLA Ops:
  0.0 1.3 %shard_map.127 = (bf16[1024,256]{1,0:T(8,128)(2,1)S(1)}, bf16[128,128]{1,0:T(8,128)(2,1)S(1)}, f32[1,512]{1,0:T(1,128)S(1)}, bf16[3,512,128]{2,1,0:T(8,128)(2,1)S(1)}, bf16[2,128,128]{2,1,0:T(8,128)(2,1)S(1)}) custom-call(s32[1]{0:T(128)} %bitcast.half, s32[1]{0:T(128)} %bitcast.1.parity, bf16[512,512]{1,0:T(8,128)(2,1)} %refs_0_.2, ...), custom_call_target="tpu_custom_call" | custom-call | bytes 1048576 | tf_op jit(solution)/shard_map/pallas_call | solution.py:173
  1.3 16.1 %all_gather.15.whole = bf16[128,512]{1,0:T(8,128)(2,1)S(1)} all-gather(bf16[128,128]{1,0:T(8,128)(2,1)S(1)} %get-tuple-element.28), channel_id=1, replica_groups=mesh['z'=4,'y'=8,'x'=4,'h'=2,'c'=2] {'h','c'}, dimensions={1}, use_global_device_ids=true | all-gather | bytes 163840 | tf_op jit(solution)/shard_map/all_gather | solution.py:343
  17.4 0.4 shard_map.128
  17.8 0.9 %copy.17 = bf16[128,2,384]{2,1,0:T(2,128)(2,1)} copy(bf16[128,2,384]{2,0,1:T(8,128)(2,1)S(1)} %bitcast.17) | data formatting | bytes 393216 | tf_op jit(solution)/shard_map/optimization_barrier | solution.py:353
  18.6 14.3 %all-to-all-start = ((bf16[128,2,384]{2,1,0:T(2,128)(2,1)}), bf16[128,2,384]{2,1,0:T(2,128)(2,1)S(1)}, u32[]{:S(2)}, u32[]{:S(2)}) async-start(bf16[128,2,384]{2,1,0:T(2,128)(2,1)} %copy.17), calls=%async_computation | async-start | bytes 393216 | tf_op jit(solution)/shard_map/all_to_all | solution.py:356
  32.9 5.2 %collective-permute-start = (bf16[1024,256]{1,0:T(8,128)(2,1)S(1)}, bf16[1024,256]{1,0:T(8,128)(2,1)S(1)}, u32[]{:S(2)}, u32[]{:S(2)}) collective-permute-start(bf16[1024,256]{1,0:T(8,128)(2,1)S(1)} %get-tuple-element.44), channel_id=1, source_target_pairs={{0,258},{128,386},{256,2},{384,130},{2,256},{130,384},{258,0},{386... | collective-permute-start | bytes 1572872 | tf_op jit(solution)/shard_map/ppermute | solution.py:372
  38.1 1.5 %shard_map.129 = (bf16[512,256]{1,0:T(8,128)(2,1)S(1)}, bf16[512,512]{1,0:T(8,128)(2,1)S(1)}, bf16[128,512]{1,0:T(8,128)(2,1)S(1)}, f32[3,3,128]{2,1,0:T(4,128)S...) custom-call(s32[1]{0:T(128)} %bitcast.half, ...), custom_call_target="tpu_custom_call" | custom-call | bytes 1048576 | tf_op jit(solution)/shard_map/pallas_call | solution.py:173
  39.6 0.0 all-to-all-done
  39.6 1.8 %shard_map.130 = bf16[128,128]{1,0:T(8,128)(2,1)S(1)} custom-call(s32[1]{0:T(128)} %bitcast.5.mine, f32[3,3,128]{2,1,0:T(4,128)S(1)} %get-tuple-element.37.short_w, f32[2,128]{1,0:T(2,128)S(1)} %get-tuple-element.38.bias, bf16[2,128,384]{2,1,0:T(8,128)(2,1)S(1)} %bitcast.18, bf16[128,128]{1,0:T(8,128)(2,1)S(1)} %get-tuple-element.40.previous, ...), custom_call_target="tpu_custom_call" | custom-call | flops 536870912 | bytes 1048576 | tf_op jit(solution)/shard_map/pallas_call | solution.py:173
  41.5 0.7 copy.19
  42.2 17.9 %all-to-all-start.1 = ((bf16[256,1,128]{2,1,0:T(2,128)(2,1)}), bf16[256,1,128]{2,1,0:T(2,128)(2,1)S(1)}, u32[]{:S(2)}, u32[]{:S(2)}) async-start(bf16[256,1,128]{2,1,0:T(2,128)(2,1)} %copy.19), calls=%async_computation.1 | async-start | bytes 262144 | tf_op jit(solution)/shard_map/all_to_all | solution.py:386
  60.1 2.9 %collective-permute-done.near = bf16[1024,256]{1,0:T(8,128)(2,1)S(1)} collective-permute-done((bf16[1024,256]{1,0:T(8,128)(2,1)S(1)}, bf16[1024,256]{1,0:T(8,128)(2,1)S(1)}, u32[]{:S(2)}, u32[]{:S(2)}) %collective-permute-start) | collective-permute-done | bytes 524320 | tf_op jit(solution)/shard_map/ppermute | solution.py:372
  63.0 2.5 %collective-permute-start.1 = (bf16[768,256]{1,0:T(8,128)(2,1)S(1)}, bf16[768,256]{1,0:T(8,128)(2,1)S(1)}, u32[]{:S(2)}, u32[]{:S(2)}) collective-permute-start(bf16[768,256]{1,0:T(8,128)(2,1)S(1)} %slice.4), channel_id=1, source_target_pairs={{0,16},{1,5},{4,20},{5,1},{8,24},{9,13},{12,28},{13,9},{16,0},{17,... | collective-permute-start | bytes 1179656 | tf_op jit(solution)/shard_map/ppermute | solution.py:373
  65.6 0.0 all-to-all-done.1
  65.6 0.3 shard_map.131
  65.9 6.0 %all-gather = f32[256,512]{1,0:T(8,128)S(1)} all-gather(f32[128,512]{1,0:T(8,128)S(1)} %shard_map.131), channel_id=2, replica_groups=mesh['z'=4,'y'=8,'x'=4,'h'=2,'c'=2] {'c'}, dimensions={0}, use_global_device_ids=true | all-gather | bytes 786432 | tf_op jit(solution)/shard_map/all_gather | solution.py:404
  71.8 0.6 shard_map.132
  72.4 0.0 collective-permute-done.1.far
  72.4 0.4 shard_map.133
  72.8 2.8 %all-gather.1 = bf16[4,128,128]{2,1,0:T(8,128)(2,1)S(1)} all-gather(bf16[2,128,128]{2,1,0:T(8,128)(2,1)S(1)} %shard_map.133), channel_id=3, replica_groups=mesh['z'=4,'y'=8,'x'=4,'h'=2,'c'=2] {'c'}, dimensions={0}, use_global_device_ids=true | all-gather | bytes 196608 | tf_op jit(solution)/shard_map/all_gather | solution.py:425
  75.6 0.6 add_convert_fusion
  (5 shorter events, 0.1 us)
Async XLA Ops:
  18.6 21.0 %all-to-all-start = ((bf16[128,2,384]{2,1,0:T(2,128)(2,1)}), bf16[128,2,384]{2,1,0:T(2,128)(2,1)S(1)}, u32[]{:S(2)}, u32[]{:S(2)}) async-start(bf16[128,2,384]{2,1,0:T(2,128)(2,1)} %copy.17), calls=%async_computation | async-start | bytes 393216 | tf_op jit(solution)/shard_map/all_to_all | solution.py:356
  32.9 30.1 %collective-permute-start = (bf16[1024,256]{1,0:T(8,128)(2,1)S(1)}, bf16[1024,256]{1,0:T(8,128)(2,1)S(1)}, u32[]{:S(2)}, u32[]{:S(2)}) collective-permute-start(bf16[1024,256]{1,0:T(8,128)(2,1)S(1)} %get-tuple-element.44), channel_id=1, source_target_pairs={{0,258},{128,386},{256,2},{384,130},{2,256},{130,384},{258,0},{386... | collective-permute-start | bytes 1572872 | tf_op jit(solution)/shard_map/ppermute | solution.py:372
  42.2 23.4 %all-to-all-start.1 = ((bf16[256,1,128]{2,1,0:T(2,128)(2,1)}), bf16[256,1,128]{2,1,0:T(2,128)(2,1)S(1)}, u32[]{:S(2)}, u32[]{:S(2)}) async-start(bf16[256,1,128]{2,1,0:T(2,128)(2,1)} %copy.19), calls=%async_computation.1 | async-start | bytes 262144 | tf_op jit(solution)/shard_map/all_to_all | solution.py:386
  63.0 9.4 %collective-permute-start.1 = (bf16[768,256]{1,0:T(8,128)(2,1)S(1)}, bf16[768,256]{1,0:T(8,128)(2,1)S(1)}, u32[]{:S(2)}, u32[]{:S(2)}) collective-permute-start(bf16[768,256]{1,0:T(8,128)(2,1)S(1)} %slice.4), channel_id=1, source_target_pairs={{0,16},{1,5},{4,20},{5,1},{8,24},{9,13},{12,28},{13,9},{16,0},{17,... | collective-permute-start | bytes 1179656 | tf_op jit(solution)/shard_map/ppermute | solution.py:373

commit v6 on v5

--- a/solution.py
+++ b/solution.py
@@ -260,14 +260,14 @@
         )
         for k in range(2)
     ]
-    partial[...] = parts[0] + parts[1]
+    partial[...] = (parts[0] + parts[1]).astype(partial.dtype)
 
 
 def mlp_kernel(place, whole, shares, gain, w_up, w_down, near, own, normed, partial):
     units = whole.shape[1]
     width = own.shape[1]
     half_units = units // 2
-    share = shares[0] + shares[1]
+    share = shares[0].astype(jnp.float32) + shares[1].astype(jnp.float32)
     middle = (whole[...].astype(jnp.float32) + share).astype(jnp.bfloat16)
     mine = middle[:, :width]
     for k in range(1, units // width):
@@ -393,7 +393,7 @@
     )
     partial = call(
         out_kernel,
-        shape((samples, blocks * width), jnp.float32),
+        shape((samples, blocks * width), jnp.bfloat16),
         2**31,
         half,
         returned.reshape(2, shards, samples),

time: 76.6 us -> 76.6 us (level)
  no operation moved by 1% of the time
where the time goes in v6:
time: 76.6 us; the launch traced here: 76.3 us
  starting transfers between devices  39.9 us (52%)
  blocking collectives  24.8 us (32%)
  Pallas kernels  6.21 us (8%)
  waiting for transfers between devices  2.87 us (4%)
  local copies, waits for them, and re-layouts  1.68 us (2%)
    all_to_all x1, starting transfers between devices, local(): lax.all_to_all(doubled, ('h',) + SEQ, split_axis=0, concat_axis=0, tiled=...  17.9 us
    all_gather x1, blocking collectives, local(): whole = lax.all_gather(tokens, CH, axis=1, tiled=True)  16.1 us
    all_to_all x1, starting transfers between devices, local(): lax.all_to_all(outgoing, SEQ, split_axis=0, concat_axis=0, tiled=True, ax...  14.3 us
    pallas_call x7, Pallas kernels, call(): pl.pallas_call(kernel, out_shape=out_shape, in_specs=[smem] * scalars + [...  6.21 us
    all_gather x1, blocking collectives, local(): shares = lax.all_gather(partial, 'c', axis=0)  5.79 us
    ppermute x1, starting transfers between devices, local(): near = lax.ppermute(sent, ('z', 'h'), other_half_pairs())  5.18 us
    all_gather x1, blocking collectives, local(): pieces = lax.all_gather(pieces, 'c', axis=0)  2.98 us
    ppermute x1, waiting for transfers between devices, local(): near = lax.ppermute(sent, ('z', 'h'), other_half_pairs())  2.86 us
  transfers between devices with their start and end apart: 4, of which 1 were waited for; matrix products, arithmetic and copies ran while one was open for 1% of the time, Pallas kernels for 5%

profile of v6, /device:TPU:1, one launch (start us, length us, event | category | flops | bytes accessed | tf_op | source)
XLA Modules:
  0.0 76.3 jit_solution(12210364377973263720)
XLA Ops:
  0.0 1.3 %shard_map.127 = (bf16[1024,256]{1,0:T(8,128)(2,1)S(1)}, bf16[128,128]{1,0:T(8,128)(2,1)S(1)}, f32[1,512]{1,0:T(1,128)S(1)}, bf16[3,512,128]{2,1,0:T(8,128)(2,1)S(1)}, bf16[2,128,128]{2,1,0:T(8,128)(2,1)S(1)}) custom-call(s32[1]{0:T(128)} %bitcast.half, s32[1]{0:T(128)} %bitcast.1.parity, bf16[512,512]{1,0:T(8,128)(2,1)} %refs_0_.2, ...), custom_call_target="tpu_custom_call" | custom-call | bytes 1048576 | tf_op jit(solution)/shard_map/pallas_call | solution.py:173
  1.3 16.1 %all_gather.15.whole = bf16[128,512]{1,0:T(8,128)(2,1)S(1)} all-gather(bf16[128,128]{1,0:T(8,128)(2,1)S(1)} %get-tuple-element.28), channel_id=1, replica_groups=mesh['z'=4,'y'=8,'x'=4,'h'=2,'c'=2] {'h','c'}, dimensions={1}, use_global_device_ids=true | all-gather | bytes 163840 | tf_op jit(solution)/shard_map/all_gather | solution.py:343
  17.4 0.4 shard_map.128
  17.8 0.9 %copy.17 = bf16[128,2,384]{2,1,0:T(2,128)(2,1)} copy(bf16[128,2,384]{2,0,1:T(8,128)(2,1)S(1)} %bitcast.17) | data formatting | bytes 393216 | tf_op jit(solution)/shard_map/optimization_barrier | solution.py:353
  18.6 14.3 %all-to-all-start = ((bf16[128,2,384]{2,1,0:T(2,128)(2,1)}), bf16[128,2,384]{2,1,0:T(2,128)(2,1)S(1)}, u32[]{:S(2)}, u32[]{:S(2)}) async-start(bf16[128,2,384]{2,1,0:T(2,128)(2,1)} %copy.17), calls=%async_computation | async-start | bytes 393216 | tf_op jit(solution)/shard_map/all_to_all | solution.py:356
  32.9 5.2 %collective-permute-start = (bf16[1024,256]{1,0:T(8,128)(2,1)S(1)}, bf16[1024,256]{1,0:T(8,128)(2,1)S(1)}, u32[]{:S(2)}, u32[]{:S(2)}) collective-permute-start(bf16[1024,256]{1,0:T(8,128)(2,1)S(1)} %get-tuple-element.44), channel_id=1, source_target_pairs={{0,258},{128,386},{256,2},{384,130},{2,256},{130,384},{258,0},{386... | collective-permute-start | bytes 1572872 | tf_op jit(solution)/shard_map/ppermute | solution.py:372
  38.1 1.5 %shard_map.129 = (bf16[512,256]{1,0:T(8,128)(2,1)S(1)}, bf16[512,512]{1,0:T(8,128)(2,1)S(1)}, bf16[128,512]{1,0:T(8,128)(2,1)S(1)}, f32[3,3,128]{2,1,0:T(4,128)S...) custom-call(s32[1]{0:T(128)} %bitcast.half, ...), custom_call_target="tpu_custom_call" | custom-call | bytes 1048576 | tf_op jit(solution)/shard_map/pallas_call | solution.py:173
  39.6 0.0 all-to-all-done
  39.6 1.8 %shard_map.130 = bf16[128,128]{1,0:T(8,128)(2,1)S(1)} custom-call(s32[1]{0:T(128)} %bitcast.5.mine, f32[3,3,128]{2,1,0:T(4,128)S(1)} %get-tuple-element.37.short_w, f32[2,128]{1,0:T(2,128)S(1)} %get-tuple-element.38.bias, bf16[2,128,384]{2,1,0:T(8,128)(2,1)S(1)} %bitcast.18, bf16[128,128]{1,0:T(8,128)(2,1)S(1)} %get-tuple-element.40.previous, ...), custom_call_target="tpu_custom_call" | custom-call | flops 536870912 | bytes 1048576 | tf_op jit(solution)/shard_map/pallas_call | solution.py:173
  41.5 0.7 copy.19
  42.2 17.9 %all-to-all-start.1 = ((bf16[256,1,128]{2,1,0:T(2,128)(2,1)}), bf16[256,1,128]{2,1,0:T(2,128)(2,1)S(1)}, u32[]{:S(2)}, u32[]{:S(2)}) async-start(bf16[256,1,128]{2,1,0:T(2,128)(2,1)} %copy.19), calls=%async_computation.1 | async-start | bytes 262144 | tf_op jit(solution)/shard_map/all_to_all | solution.py:386
  60.1 2.9 %collective-permute-done.near = bf16[1024,256]{1,0:T(8,128)(2,1)S(1)} collective-permute-done((bf16[1024,256]{1,0:T(8,128)(2,1)S(1)}, bf16[1024,256]{1,0:T(8,128)(2,1)S(1)}, u32[]{:S(2)}, u32[]{:S(2)}) %collective-permute-start) | collective-permute-done | bytes 524320 | tf_op jit(solution)/shard_map/ppermute | solution.py:372
  63.0 2.5 %collective-permute-start.1 = (bf16[768,256]{1,0:T(8,128)(2,1)S(1)}, bf16[768,256]{1,0:T(8,128)(2,1)S(1)}, u32[]{:S(2)}, u32[]{:S(2)}) collective-permute-start(bf16[768,256]{1,0:T(8,128)(2,1)S(1)} %slice.4), channel_id=1, source_target_pairs={{0,16},{1,5},{4,20},{5,1},{8,24},{9,13},{12,28},{13,9},{16,0},{17,... | collective-permute-start | bytes 1179656 | tf_op jit(solution)/shard_map/ppermute | solution.py:373
  65.6 0.0 all-to-all-done.1
  65.6 0.3 shard_map.131
  65.9 5.8 %all-gather = bf16[256,512]{1,0:T(8,128)(2,1)S(1)} all-gather(bf16[128,512]{1,0:T(8,128)(2,1)S(1)} %shard_map.131), channel_id=2, replica_groups=mesh['z'=4,'y'=8,'x'=4,'h'=2,'c'=2] {'c'}, dimensions={0}, use_global_device_ids=true | all-gather | bytes 393216 | tf_op jit(solution)/shard_map/all_gather | solution.py:404
  71.7 0.6 shard_map.132
  72.3 0.0 collective-permute-done.1.far
  72.3 0.4 shard_map.133
  72.6 3.0 %all-gather.1 = bf16[4,128,128]{2,1,0:T(8,128)(2,1)S(1)} all-gather(bf16[2,128,128]{2,1,0:T(8,128)(2,1)S(1)} %shard_map.133), channel_id=3, replica_groups=mesh['z'=4,'y'=8,'x'=4,'h'=2,'c'=2] {'c'}, dimensions={0}, use_global_device_ids=true | all-gather | bytes 196608 | tf_op jit(solution)/shard_map/all_gather | solution.py:425
  75.6 0.6 add_convert_fusion
  (5 shorter events, 0.1 us)
Async XLA Ops:
  18.6 21.0 %all-to-all-start = ((bf16[128,2,384]{2,1,0:T(2,128)(2,1)}), bf16[128,2,384]{2,1,0:T(2,128)(2,1)S(1)}, u32[]{:S(2)}, u32[]{:S(2)}) async-start(bf16[128,2,384]{2,1,0:T(2,128)(2,1)} %copy.17), calls=%async_computation | async-start | bytes 393216 | tf_op jit(solution)/shard_map/all_to_all | solution.py:356
  32.9 30.1 %collective-permute-start = (bf16[1024,256]{1,0:T(8,128)(2,1)S(1)}, bf16[1024,256]{1,0:T(8,128)(2,1)S(1)}, u32[]{:S(2)}, u32[]{:S(2)}) collective-permute-start(bf16[1024,256]{1,0:T(8,128)(2,1)S(1)} %get-tuple-element.44), channel_id=1, source_target_pairs={{0,258},{128,386},{256,2},{384,130},{2,256},{130,384},{258,0},{386... | collective-permute-start | bytes 1572872 | tf_op jit(solution)/shard_map/ppermute | solution.py:372
  42.2 23.4 %all-to-all-start.1 = ((bf16[256,1,128]{2,1,0:T(2,128)(2,1)}), bf16[256,1,128]{2,1,0:T(2,128)(2,1)S(1)}, u32[]{:S(2)}, u32[]{:S(2)}) async-start(bf16[256,1,128]{2,1,0:T(2,128)(2,1)} %copy.19), calls=%async_computation.1 | async-start | bytes 262144 | tf_op jit(solution)/shard_map/all_to_all | solution.py:386
  63.0 9.2 %collective-permute-start.1 = (bf16[768,256]{1,0:T(8,128)(2,1)S(1)}, bf16[768,256]{1,0:T(8,128)(2,1)S(1)}, u32[]{:S(2)}, u32[]{:S(2)}) collective-permute-start(bf16[768,256]{1,0:T(8,128)(2,1)S(1)} %slice.4), channel_id=1, source_target_pairs={{0,16},{1,5},{4,20},{5,1},{8,24},{9,13},{12,28},{13,9},{16,0},{17,... | collective-permute-start | bytes 1179656 | tf_op jit(solution)/shard_map/ppermute | solution.py:373

commit v7 on v4

--- a/solution.py
+++ b/solution.py
@@ -27,12 +27,15 @@
 
 
 def first_ranks(deep, high, wide):
-    return [
-        ((deep - 1 - z) * high + (y + high // 2) % high) * wide + (x + wide - 1) % wide
-        for z in range(deep)
-        for y in range(high)
-        for x in range(wide)
-    ]
+    def nearness(place):
+        y = abs(place // wide % high - high // 2)
+        x = abs(place % wide - (wide - 1))
+        z = deep - 1 - place // (high * wide)
+        return -(z + min(y, high - y) + min(x, wide - x))
+
+    last = ((deep - 1) * high + high // 2) * wide + wide - 1
+    rest = [place for place in range(deep * high * wide) if place != last]
+    return [last] + sorted(rest, key=nearness)
 
 
 def second_ranks(deep, high, wide):
@@ -313,10 +316,288 @@
     shards = lax.axis_size(SEQ)
     blocks = lax.axis_size(CH)
     shape = jax.ShapeDtypeStruct
+    ranks = first_ranks(deep, high, wide)
+    return [len(ranks) + rank for rank in ranks] + ranks
+
+
+def previous_rows(times):
+    times = np.asarray(times)
+    return (times[:, None] == times[None, :] + 1).astype(ml_dtypes.bfloat16)
+
+
+def transform_tables(rows, cols, times):
+    size = rows * cols
+    times = np.asarray(times)
+    row = np.arange(rows, dtype=np.float64)
+    col = np.arange(cols, dtype=np.float64)
+    outer_angle = 2.0 * np.pi * (((row[:, None] + 0.25) * row[None, :]) % rows) / rows
+    inner_angle = 2.0 * np.pi * ((col[:, None] * col[None, :]) % cols) / cols
+    turn_angle = 2.0 * np.pi * (row[:, None] + 0.25) * col[None, :] / size
+    outer = np.concatenate([np.cos(outer_angle), -np.sin(outer_angle)], axis=0)
+    cos, sin = np.cos(inner_angle), np.sin(inner_angle)
+    inner = np.block([[cos, -sin], [sin, cos]])
+    outer = outer[:, times]
+    outer_high, outer_low = halves_of(outer)
+    inner_high, inner_low = halves_of(inner)
+    back_high, back_low = halves_of(outer.T / size)
+    products = [np.concatenate([outer_high, outer_low], axis=1)]
+    products += [inner_high, inner_low, np.concatenate([back_high, back_low], axis=0)]
+    turn = np.stack([np.cos(turn_angle), -np.sin(turn_angle)])
+    return np.stack(products), turn.astype(np.float32)
+
+
+def dot(left, right):
+    return jnp.dot(left, right, preferred_element_type=jnp.float32)
+
+
+def split(values):
+    high = values.astype(jnp.bfloat16)
+    return high, (values - high.astype(jnp.float32)).astype(jnp.bfloat16)
+
+
+def dot_split(values, high_table, low_table):
+    high, low = split(values)
+    rows = values.shape[0]
+    both = dot(jnp.concatenate([high, low], axis=0), high_table)
+    return both[:rows] + both[rows:] + dot(high, low_table)
+
+
+def delayed(values, above, by):
+    col = lax.broadcasted_iota(jnp.int32, values.shape, 1)
+    return jnp.where(col >= by, pltpu.roll(values, by, 1), pltpu.roll(above, by, 1))
+
+
+def round_bf16(values):
+    return values.astype(jnp.bfloat16).astype(jnp.float32)
+
+
+def channel_kernel(mine, short_w, bias, u, previous, products, turn, mixed):
+    rows, cols = u.shape[1], u.shape[2] // 3
+    projected = u[0]
+    above = dot(previous[...], projected)
+    outer, inner_high, inner_low = products[0], products[1], products[2]
+    back_high, back_low = products[3, :rows], products[3, rows:]
+    turn_real, turn_imag = turn[0], turn[1]
+    per_channel = jnp.concatenate([short_w[k] for k in range(short_w.shape[0])] + [bias[...]], axis=0)
+    column = lax.broadcasted_iota(jnp.int32, per_channel.shape, 1)
+    scalars = jnp.sum(jnp.where(column == mine[0], per_channel, 0.0), axis=1, keepdims=True)
+    scalars = [scalars[k : k + 1] for k in range(scalars.shape[0])]
+
+    def short(k):
+        values = projected[:, k * cols : (k + 1) * cols].astype(jnp.float32)
+        total = scalars[3 * k] * values
+        past = above[:, k * cols : (k + 1) * cols]
+        total = total + scalars[3 * k + 1] * delayed(values, past, 1)
+        total = total + scalars[3 * k + 2] * delayed(values, past, 2)
+        return total.astype(jnp.bfloat16)
+
+    def forward(signals):
+        count = len(signals)
+        side = jnp.concatenate(signals, axis=1) if count > 1 else signals[0]
+        first = dot(outer, jnp.concatenate([side, side], axis=0))
+        turned = []
+        for k in range(count):
+            real = first[:rows, k * cols : (k + 1) * cols]
+            imag = first[rows:, k * cols : (k + 1) * cols]
+            turned.append(
+                jnp.concatenate(
+                    [
+                        real * turn_real - imag * turn_imag,
+                        real * turn_imag + imag * turn_real,
+                    ],
+                    axis=1,
+                )
+            )
+        stacked = jnp.concatenate(turned, axis=0) if count > 1 else turned[0]
+        spectra = dot_split(stacked, inner_high, inner_low)
+        return [
+            (spectra[k * rows : (k + 1) * rows, :cols], spectra[k * rows : (k + 1) * rows, cols:])
+            for k in range(count)
+        ]
+
+    def inverse(one, two):
+        real = one[0] * two[0] - one[1] * two[1]
+        negated = -one[0] * two[1] - one[1] * two[0]
+        inner = dot_split(
+            jnp.concatenate([real, negated], axis=1), inner_high, inner_low
+        )
+        real, negated = inner[:, :cols], inner[:, cols:]
+        turned = jnp.concatenate(
+            [
+                real * turn_real - negated * turn_imag,
+                -negated * turn_real - real * turn_imag,
+            ],
+            axis=0,
+        )
+        high, low = split(turned)
+        side = dot(back_high, jnp.concatenate([high, low], axis=1))
+        return side[:, :cols] + side[:, cols:] + dot(back_low, high)
+
+    v = short(0)
+    signal, response_one, response_two = forward([v, u[1, :, :cols], u[1, :, cols : 2 * cols]])
+    first = inverse(signal, response_one) + scalars[9] * v.astype(jnp.float32)
+    gated = (short(1).astype(jnp.float32) * round_bf16(first)).astype(jnp.bfloat16)
+    (signal,) = forward([gated])
+    second = inverse(signal, response_two) + scalars[10] * gated.astype(jnp.float32)
+    mixed[...] = (short(2).astype(jnp.float32) * round_bf16(second)).astype(jnp.bfloat16)
+
+
+def call(
+    kernel, out_shape, flops, *operands, scalars=0, source=pltpu.VMEM, scratch=(), limit=16
+):
+    vmem = pl.BlockSpec(memory_space=pltpu.VMEM)
+    smem = pl.BlockSpec(memory_space=pltpu.SMEM)
+    held = pl.BlockSpec(memory_space=source)
+    return pl.pallas_call(
+        kernel,
+        out_shape=out_shape,
+        in_specs=[smem] * scalars + [held] * (len(operands) - scalars),
+        out_specs=jax.tree.map(lambda _: vmem, out_shape),
+        scratch_shapes=scratch,
+        compiler_params=pltpu.CompilerParams(vmem_limit_bytes=limit * 2**20),
+        cost_estimate=pl.CostEstimate(flops=flops, bytes_accessed=2**20, transcendentals=0),
+    )(*operands)
+
+
+def copy_all(pairs, sems):
+    copies = [
+        pltpu.make_async_copy(source, target, sems.at[k])
+        for k, (source, target) in enumerate(pairs)
+    ]
+    for copy in copies:
+        copy.start()
+    for copy in copies:
+        copy.wait()
+
+
+def first_load_kernel(half, parity, *refs):
+    count = (len(refs) + 1) // 2
+    sources, (sent, *held), sems = refs[:count], refs[count:-1], refs[-1]
+    w_up, w_down, w_out = sources[:3]
+    units, wide = w_up.shape
+    rows = w_out.shape[0]
+    part = wide // 2
+    there = pl.ds(pl.multiple_of((1 - half[0]) * part, part), part)
+    turn = pl.ds(pl.multiple_of(parity[0] * part, part), part)
+    pairs = [
+        (w_up.at[:, turn], sent.at[pl.ds(0, units)]),
+        (w_down.at[turn, there], sent.at[pl.ds(units, part)]),
+        (w_out.at[:, pl.ds(0, part)], sent.at[pl.ds(units + part, rows)]),
+        (w_out.at[:, pl.ds(part, part)], sent.at[pl.ds(units + part + rows, rows)]),
+    ]
+    copy_all(pairs + list(zip(sources[3:], held)), sems)
+
+
+def last_load_kernel(half, w_down, *refs):
+    count = (len(refs) - 2) // 2
+    sources, (down, *held), sems = refs[:count], refs[count:-1], refs[-1]
+    part = down.shape[1]
+    here = pl.ds(pl.multiple_of(half[0] * part, part), part)
+    copy_all([(w_down.at[:, here], down)] + list(zip(sources, held)), sems)
+
+
+def load(kernel, copies, cut, scalars, *arrays):
+    arrays = [pltpu.with_memory_space_constraint(array, pltpu.HBM) for array in arrays]
+    held = [pltpu.VMEM(cut, jnp.bfloat16)]
+    held += [pltpu.VMEM(array.shape, array.dtype) for array in arrays[-(copies - 1) :]]
+    sems = [pltpu.SemaphoreType.DMA((len(arrays) + 1,))]
+    return call(
+        kernel,
+        held,
+        0,
+        *scalars,
+        *arrays,
+        scalars=len(scalars),
+        source=pltpu.HBM,
+        scratch=sems,
+    )
+
+
+def project_kernel(whole, gain, w_in, filters, outgoing):
+    normed = rms_norm(whole[...], gain[...])
+    count, _, width = w_in.shape
+    for k in range(count):
+        outgoing[0, :, k * width : (k + 1) * width] = lax.dot_general(
+            w_in[k], normed, (((0,), (1,)), ((), ())), preferred_element_type=jnp.float32
+        ).astype(jnp.bfloat16)
+    outgoing[1] = jnp.concatenate([filters[0], filters[1], jnp.zeros_like(filters[0])], axis=1)
+
+
+def out_kernel(half, arrived, own, near, partial):
+    rows = arrived.shape[1]
+    first = near.shape[0] - 2 * rows
+    other = jnp.concatenate([near[first : first + rows], near[first + rows :]], axis=1)
+    low = half[0] == 0
+    weights = (jnp.where(low, own[...], other), jnp.where(low, other, own[...]))
+    parts = [
+        lax.dot_general(
+            arrived[1 - k],
+            weights[k],
+            (((0,), (0,)), ((), ())),
+            preferred_element_type=jnp.float32,
+        )
+        for k in range(2)
+    ]
+    partial[...] = parts[0] + parts[1]
+
+
+def mlp_kernel(place, whole, shares, gain, w_up, w_down, near, own, normed, partial):
+    units = whole.shape[1]
+    width = own.shape[1]
+    half_units = units // 2
+    share = shares[0] + shares[1]
+    middle = (whole[...].astype(jnp.float32) + share).astype(jnp.bfloat16)
+    mine = middle[:, :width]
+    for k in range(1, units // width):
+        mine = jnp.where(place[0] == k, middle[:, k * width : (k + 1) * width], mine)
+    own[...] = mine
+    scaled = rms_norm(middle, gain[...])
+    normed[...] = scaled
+    hidden = jax.nn.gelu(dot(scaled, w_up[...])).astype(jnp.bfloat16)
+    total = dot(hidden, w_down[...])
+    hidden = jax.nn.gelu(dot(scaled, near[:units])).astype(jnp.bfloat16)
+    partial[...] = total + dot(hidden, near[units : units + half_units])
+
+
+def far_kernel(normed, partial, far, pieces):
+    count, _, width = pieces.shape
+    units = normed.shape[1]
+    hidden = jax.nn.gelu(dot(normed[...], far[:units])).astype(jnp.bfloat16)
+    total = (partial[...] + dot(hidden, far[units:])).astype(jnp.bfloat16)
+    for k in range(count):
+        pieces[k] = total[:, k * width : (k + 1) * width]
+
+
+def other_half_pairs():
+    pairs = []
+    for z in range(8):
+        there = (z + 2) % 8
+        if there // 4 == z // 4:
+            there = (z - 2) % 8
+        pairs.append((z % 4 * 2 + z // 4, there % 4 * 2 + there // 4))
+    return pairs
+
+
+def neighbour_pairs():
+    high, wide = lax.axis_size("y"), lax.axis_size("x")
+    pairs = []
+    for y in range(high):
+        for x in range(wide):
+            pairs.append(((y * wide + x) * 2, ((y ^ 1) * wide + x) * 2))
+            pairs.append(((y * wide + x) * 2 + 1, (y * wide + (x ^ 1)) * 2 + 1))
+    return pairs
+
+
+def local(tokens, gain_mix, w_in, short_w, filters, conv_bias, w_out, gain_mlp, w_up, w_down):
+    samples, width = tokens.shape
+    shards = lax.axis_size(SEQ)
+    blocks = lax.axis_size(CH)
+    shape = jax.ShapeDtypeStruct
     place_z, place_y, place_x = (lax.axis_index(axis) for axis in SEQ)
     mine = (DEEP - 1 - place_z) * HIGH + (place_y + HIGH // 2) % HIGH
     mine = (mine * WIDE + (place_x + 1) % WIDE).astype(jnp.int32)[None]
     ranks = first_ranks(DEEP, HIGH, WIDE)
+    mine = jnp.asarray(np.argsort(ranks).astype(np.int32))[lax.axis_index(SEQ)][None]
     place = lax.axis_index(CH).astype(jnp.int32)[None]
     half = lax.axis_index("h").astype(jnp.int32)[None]
     side = jnp.where(lax.axis_index("c") == 0, lax.axis_index("y"), lax.axis_index("x"))
@@ -348,8 +629,8 @@
         w_in,
         filters,
     )
-    outgoing, sent, half, parity, place, mine, w_up = lax.optimization_barrier(
-        (outgoing.transpose(1, 0, 2), sent, half, parity, place, mine, w_up)
+    outgoing, sent, half, parity, place, w_up = lax.optimization_barrier(
+        (outgoing.transpose(1, 0, 2), sent, half, parity, place, w_up)
     )
     arrived = lax.all_to_all(
         outgoing, SEQ, split_axis=0, concat_axis=0, tiled=True, axis_index_groups=[ranks]

time: 76.3 us -> 76.6 us (level)
  starting transfers between devices: 39.9 us -> 38.5 us
  local copies, waits for them, and re-layouts: 1.68 us -> 2.92 us
    all_to_all x1, waiting for transfers between devices: 0.01 us -> 1.7 us  [local(): lax.all_to_all(doubled, ('h',) + SEQ, split_axis=0, concat_axis=0, tiled=...]
    all_to_all x1, starting transfers between devices: 17.9 us -> 16.4 us  [local(): lax.all_to_all(doubled, ('h',) + SEQ, split_axis=0, concat_axis=0, tiled=...]
    all_gather x1, blocking collectives: 6.49 us -> 5.08 us  [local(): shares = lax.all_gather(partial, 'c', axis=0)]
    ppermute x1, waiting for transfers between devices: 2.35 us -> 1.08 us  [local(): near = lax.ppermute(sent, ('z', 'h'), other_half_pairs())]
    all_gather x1, blocking collectives: 2.36 us -> 3.17 us  [local(): pieces = lax.all_gather(pieces, 'c', axis=0)]
    all_to_all x1, starting transfers between devices: 14.3 us -> 13.5 us  [local(): lax.all_to_all(outgoing, SEQ, split_axis=0, concat_axis=0, tiled=True, ax...]
  transfers between devices with their start and end apart: 4 -> 4, of which waited for: 1 -> 2; matrix products, arithmetic and copies ran while one was open for 1% -> 2% of each run, Pallas kernels for 6% -> 6%
where the time goes in v7:
time: 76.6 us; the launch traced here: 76.2 us
  starting transfers between devices  38.5 us (50%)
  blocking collectives  24.3 us (32%)
  Pallas kernels  6.92 us (9%)
  local copies, waits for them, and re-layouts  2.92 us (4%)
  waiting for transfers between devices  2.79 us (4%)
    all_to_all x1, starting transfers between devices, local(): lax.all_to_all(doubled, ('h',) + SEQ, split_axis=0, concat_axis=0, tiled=...  16.4 us
    all_gather x1, blocking collectives, local(): whole = lax.all_gather(tokens, CH, axis=1, tiled=True)  16.1 us
    all_to_all x1, starting transfers between devices, local(): lax.all_to_all(outgoing, SEQ, split_axis=0, concat_axis=0, tiled=True, ax...  13.5 us
    pallas_call x7, Pallas kernels, call(): pl.pallas_call(kernel, out_shape=out_shape, in_specs=[smem] * scalars + [...  6.92 us
    ppermute x1, starting transfers between devices, local(): near = lax.ppermute(sent, ('z', 'h'), other_half_pairs())  5.84 us
    all_gather x1, blocking collectives, local(): shares = lax.all_gather(partial, 'c', axis=0)  5.08 us
    all_gather x1, blocking collectives, local(): pieces = lax.all_gather(pieces, 'c', axis=0)  3.17 us
    ppermute x1, starting transfers between devices, local(): lax.ppermute(near[:width * blocks * 3 // 2], ('y', 'x', 'c'), neighbour_p...  2.78 us
  transfers between devices with their start and end apart: 4, of which 2 were waited for; matrix products, arithmetic and copies ran while one was open for 2% of the time, Pallas kernels for 6%

profile of v7, /device:TPU:1, one launch (start us, length us, event | category | flops | bytes accessed | tf_op | source)
XLA Modules:
  0.0 76.2 jit_solution(289871023914084926)
XLA Ops:
  0.0 1.3 %shard_map.136 = (bf16[1024,256]{1,0:T(8,128)(2,1)S(1)}, bf16[128,128]{1,0:T(8,128)(2,1)S(1)}, f32[1,512]{1,0:T(1,128)S(1)}, bf16[3,512,128]{2,1,0:T(8,128)(2,1)S(1)}, bf16[2,128,128]{2,1,0:T(8,128)(2,1)S(1)}) custom-call(s32[1]{0:T(128)} %bitcast.half, s32[1]{0:T(128)} %bitcast.1.parity, bf16[512,512]{1,0:T(8,128)(2,1)} %refs_0_.2, ...), custom_call_target="tpu_custom_call" | custom-call | bytes 1048576 | tf_op jit(solution)/shard_map/pallas_call | solution.py:451
  1.3 16.1 %all_gather.15.whole = bf16[128,512]{1,0:T(8,128)(2,1)S(1)} all-gather(bf16[128,128]{1,0:T(8,128)(2,1)S(1)} %get-tuple-element.27), channel_id=1, replica_groups=mesh['z'=4,'y'=8,'x'=4,'h'=2,'c'=2] {'h','c'}, dimensions={1}, use_global_device_ids=true | all-gather | bytes 163840 | tf_op jit(solution)/shard_map/all_gather | solution.py:622
  17.4 0.4 shard_map.137
  17.8 0.9 %copy.18 = bf16[128,2,384]{2,1,0:T(2,128)(2,1)} copy(bf16[128,2,384]{2,0,1:T(8,128)(2,1)S(1)} %bitcast.16) | data formatting | bytes 393216 | tf_op jit(solution)/shard_map/optimization_barrier | solution.py:632
  18.6 13.5 %all-to-all-start = ((bf16[128,2,384]{2,1,0:T(2,128)(2,1)}), bf16[128,2,384]{2,1,0:T(2,128)(2,1)S(1)}, u32[]{:S(2)}, u32[]{:S(2)}) async-start(bf16[128,2,384]{2,1,0:T(2,128)(2,1)} %copy.18), calls=%async_computation | async-start | bytes 393216 | tf_op jit(solution)/shard_map/all_to_all | solution.py:635
  32.1 5.8 %collective-permute-start = (bf16[1024,256]{1,0:T(8,128)(2,1)S(1)}, bf16[1024,256]{1,0:T(8,128)(2,1)S(1)}, u32[]{:S(2)}, u32[]{:S(2)}) collective-permute-start(bf16[1024,256]{1,0:T(8,128)(2,1)S(1)} %get-tuple-element.42), channel_id=1, source_target_pairs={{0,258},{128,386},{256,2},{384,130},{2,256},{130,384},{258,0},{386... | collective-permute-start | bytes 1572872 | tf_op jit(solution)/shard_map/ppermute | solution.py:651
  38.0 0.0 copy-start
  38.0 0.6 copy-done
  38.6 0.6 dynamic_slice.7.mine
  39.2 1.5 %shard_map.138 = (bf16[512,256]{1,0:T(8,128)(2,1)S(1)}, bf16[512,512]{1,0:T(8,128)(2,1)S(1)}, bf16[128,512]{1,0:T(8,128)(2,1)S(1)}, f32[3,3,128]{2,1,0:T(4,128)S...) custom-call(s32[1]{0:T(128)} %bitcast.half, ...), custom_call_target="tpu_custom_call" | custom-call | bytes 1048576 | tf_op jit(solution)/shard_map/pallas_call | solution.py:451
  40.7 0.0 all-to-all-done
  40.8 2.6 %shard_map.139 = bf16[128,128]{1,0:T(8,128)(2,1)S(1)} custom-call(s32[1]{0:T(128)} %dynamic_slice.7.mine, f32[3,3,128]{2,1,0:T(4,128)S(1)} %get-tuple-element.35.short_w, f32[2,128]{1,0:T(2,128)S(1)} %get-tuple-element.36.bias, bf16[2,128,384]{2,1,0:T(8,128)(2,1)S(1)} %bitcast.17, bf16[128,128]{1,0:T(8,128)(2,1)S(1)} %get-tuple-element.38.previous, ...), custom_call_target="tpu_custom_call" | custom-call | flops 536870912 | bytes 1048576 | tf_op jit(solution)/shard_map/pallas_call | solution.py:451
  43.3 0.8 copy.20
  44.1 16.4 %all-to-all-start.1 = ((bf16[256,1,128]{2,1,0:T(2,128)(2,1)}), bf16[256,1,128]{2,1,0:T(2,128)(2,1)S(1)}, u32[]{:S(2)}, u32[]{:S(2)}) async-start(bf16[256,1,128]{2,1,0:T(2,128)(2,1)} %copy.20), calls=%async_computation.1 | async-start | bytes 262144 | tf_op jit(solution)/shard_map/all_to_all | solution.py:665
  60.5 1.1 %collective-permute-done.near = bf16[1024,256]{1,0:T(8,128)(2,1)S(1)} collective-permute-done((bf16[1024,256]{1,0:T(8,128)(2,1)S(1)}, bf16[1024,256]{1,0:T(8,128)(2,1)S(1)}, u32[]{:S(2)}, u32[]{:S(2)}) %collective-permute-start) | collective-permute-done | bytes 524320 | tf_op jit(solution)/shard_map/ppermute | solution.py:651
  61.6 2.8 %collective-permute-start.1 = (bf16[768,256]{1,0:T(8,128)(2,1)S(1)}, bf16[768,256]{1,0:T(8,128)(2,1)S(1)}, u32[]{:S(2)}, u32[]{:S(2)}) collective-permute-start(bf16[768,256]{1,0:T(8,128)(2,1)S(1)} %slice.4), channel_id=1, source_target_pairs={{0,16},{1,5},{4,20},{5,1},{8,24},{9,13},{12,28},{13,9},{16,0},{17,... | collective-permute-start | bytes 1179656 | tf_op jit(solution)/shard_map/ppermute | solution.py:652
  64.4 1.7 %all-to-all-done.1 = bf16[256,1,128]{2,1,0:T(2,128)(2,1)S(1)} async-done(((bf16[256,1,128]{2,1,0:T(2,128)(2,1)}), bf16[256,1,128]{2,1,0:T(2,128)(2,1)S(1)}, u32[]{:S(2)}, u32[]{:S(2)}) %all-to-all-start.1) | async-done | bytes 65568 | tf_op jit(solution)/shard_map/all_to_all | solution.py:665
  66.1 0.2 shard_map.140
  66.4 5.1 %all-gather = f32[256,512]{1,0:T(8,128)S(1)} all-gather(f32[128,512]{1,0:T(8,128)S(1)} %shard_map.140), channel_id=2, replica_groups=mesh['z'=4,'y'=8,'x'=4,'h'=2,'c'=2] {'c'}, dimensions={0}, use_global_device_ids=true | all-gather | bytes 786432 | tf_op jit(solution)/shard_map/all_gather | solution.py:683
  71.4 0.6 shard_map.141
  72.1 0.0 collective-permute-done.1.far
  72.1 0.4 shard_map.142
  72.4 3.2 %all-gather.1 = bf16[4,128,128]{2,1,0:T(8,128)(2,1)S(1)} all-gather(bf16[2,128,128]{2,1,0:T(8,128)(2,1)S(1)} %shard_map.142), channel_id=3, replica_groups=mesh['z'=4,'y'=8,'x'=4,'h'=2,'c'=2] {'c'}, dimensions={0}, use_global_device_ids=true | all-gather | bytes 196608 | tf_op jit(solution)/shard_map/all_gather | solution.py:704
  75.6 0.6 add_convert_fusion
  (5 shorter events, 0.1 us)
Async XLA Ops:
  18.6 22.1 %all-to-all-start = ((bf16[128,2,384]{2,1,0:T(2,128)(2,1)}), bf16[128,2,384]{2,1,0:T(2,128)(2,1)S(1)}, u32[]{:S(2)}, u32[]{:S(2)}) async-start(bf16[128,2,384]{2,1,0:T(2,128)(2,1)} %copy.18), calls=%async_computation | async-start | bytes 393216 | tf_op jit(solution)/shard_map/all_to_all | solution.py:635
  32.1 29.4 %collective-permute-start = (bf16[1024,256]{1,0:T(8,128)(2,1)S(1)}, bf16[1024,256]{1,0:T(8,128)(2,1)S(1)}, u32[]{:S(2)}, u32[]{:S(2)}) collective-permute-start(bf16[1024,256]{1,0:T(8,128)(2,1)S(1)} %get-tuple-element.42), channel_id=1, source_target_pairs={{0,258},{128,386},{256,2},{384,130},{2,256},{130,384},{258,0},{386... | collective-permute-start | bytes 1572872 | tf_op jit(solution)/shard_map/ppermute | solution.py:651
  38.0 0.7 copy-start
  44.1 22.0 %all-to-all-start.1 = ((bf16[256,1,128]{2,1,0:T(2,128)(2,1)}), bf16[256,1,128]{2,1,0:T(2,128)(2,1)S(1)}, u32[]{:S(2)}, u32[]{:S(2)}) async-start(bf16[256,1,128]{2,1,0:T(2,128)(2,1)} %copy.20), calls=%async_computation.1 | async-start | bytes 262144 | tf_op jit(solution)/shard_map/all_to_all | solution.py:665
  61.6 10.5 %collective-permute-start.1 = (bf16[768,256]{1,0:T(8,128)(2,1)S(1)}, bf16[768,256]{1,0:T(8,128)(2,1)S(1)}, u32[]{:S(2)}, u32[]{:S(2)}) collective-permute-start(bf16[768,256]{1,0:T(8,128)(2,1)S(1)} %slice.4), channel_id=1, source_target_pairs={{0,16},{1,5},{4,20},{5,1},{8,24},{9,13},{12,28},{13,9},{16,0},{17,... | collective-permute-start | bytes 1179656 | tf_op jit(solution)/shard_map/ppermute | solution.py:652
